TPU v7x, 256 devices: a whole 4x4x8 slice. The times are simulated.
256 devices in a mesh: gx: 32 (over z_lo, y, core), gy: 8 (over x, z_hi).
Axes of the slice: x: 4, y: 4, z: 8 (z_hi: 2, z_lo: 4; z = z_hi * 4 + z_lo), core: 2. Of those that a mesh axis runs over, the one named last changes fastest.
Arguments:
- node_cells: int32 [3, 1048576], P(None, ('gx', 'gy')), may hold values from 0 to 191, as said below
- node_frac: float32 [3, 1048576], P(None, ('gx', 'gy')), may hold values from 0 to 1
- node_force: float32 [1048576], P(('gx', 'gy')), may hold values from -6 to 6
- node_count: int32 [256], P(('gx', 'gy')), may hold values from 1 to 4096, as said below
- z_rates: float32 [64], replicated, may hold values from 0.1 to 4
- z_synth: float32 [64, 64], replicated, may hold values from -0.75 to 0.75
- z_analysis: float32 [64, 64], replicated, may hold values from -0.75 to 0.75
Outputs:
- velocity_modes: float32 [2, 64, 1536, 1536], P(None, None, ('gx', 'gy'))
Inputs may be any that keep to these rules, and one draw needn't show every extreme that they name: `node_cells`: rows are x, y, z; x below 48, y below 192, z at most 58. `node_count`: some device holds 4096 live nodes in every draw.
All inputs are finite; a program needn't handle non-finite values.
Results may differ from a plain program's by a relative error of at most 0.003.
Values may be sent and summed in bfloat16 or wider, within the bound.
No kernel may reach another device: no remote copies, remote signals or barrier semaphores. Data moves between devices by JAX's collectives and lax.ppermute only.
A program may use at most 128 MiB of HBM per device.

v0:
```python
import math

import jax
import jax.numpy as jnp
from jax import lax
from jax.sharding import PartitionSpec as P

NX = 1536
NY = 1536
WIN = 6


node_block = 256


def shifted(block, axis, distance):
    devices = range(lax.axis_size(axis))
    route = [((i - distance) % len(devices), i) for i in devices]
    return lax.ppermute(block, axis, route)


def window_weights(frac_row, width):
    offsets = jnp.arange(width, dtype=jnp.float32)
    distance = offsets[None, :] - (width - 1) / 2.0 - frac_row[:, None]
    return jnp.exp(-distance * distance / 2.0)


def place_window(weights, lowest, extent):
    offsets = jnp.arange(weights.shape[1], dtype=jnp.int32)
    hits = (
        jnp.arange(extent, dtype=jnp.int32)[None, None, :]
        == (lowest[:, None] + offsets[None, :])[:, :, None]
    )
    return jnp.sum(jnp.where(hits, weights[:, :, None], 0.0), axis=1)


def spread_nodes(cell_rows, frac_rows, weighted, first_slot, last_slot, z_levels, wide_x, wide_y):
    capacity = weighted.shape[0]
    block_size = min(node_block, capacity)
    cells_padded = jnp.pad(cell_rows, ((0, 0), (0, block_size)))
    frac_padded = jnp.pad(frac_rows, ((0, 0), (0, block_size)))
    weight_padded = jnp.pad(weighted, (0, block_size))

    def add_block(block_index, grid_tile):
        start_slot = first_slot + block_index * block_size
        block_cells = lax.dynamic_slice_in_dim(cells_padded, start_slot, block_size, 1)
        block_frac = lax.dynamic_slice_in_dim(frac_padded, start_slot, block_size, 1)
        block_weight = lax.dynamic_slice_in_dim(weight_padded, start_slot, block_size, 0)
        live = start_slot + jnp.arange(block_size, dtype=jnp.int32) < last_slot
        amplitude = jnp.where(live, block_weight, 0.0)
        z_window = place_window(window_weights(block_frac[2], WIN), block_cells[2], z_levels)
        x_window = place_window(window_weights(block_frac[0], WIN), block_cells[0], wide_x)
        y_window = place_window(window_weights(block_frac[1], WIN), block_cells[1], wide_y)
        outer_left = ((amplitude[:, None] * z_window)[:, :, None] * x_window[:, None, :]).astype(
            jnp.bfloat16
        )
        return grid_tile + jnp.einsum(
            "nzx,ny->zxy",
            outer_left,
            y_window.astype(jnp.bfloat16),
            preferred_element_type=jnp.float32,
        )

    block_total = (jnp.maximum(last_slot - first_slot, 0) + block_size - 1) // block_size
    return lax.fori_loop(
        0, block_total, add_block, jnp.zeros((z_levels, wide_x, wide_y), jnp.float32)
    )


def fourier_last(input_real, input_imag):
    length = input_real.shape[-1]
    radix_first = 1 << math.isqrt(length).bit_length() - 1
    radix_second = length // radix_first
    leading = input_real.shape[:-1]
    highest = lax.Precision.HIGHEST

    def phase_table(rows_count, cols_count, modulus):
        phase = (
            jnp.arange(rows_count, dtype=jnp.int32)[:, None]
            * jnp.arange(cols_count, dtype=jnp.int32)[None, :]
            % modulus
        )
        angle = phase.astype(jnp.float32) * (2.0 * math.pi / modulus)
        return (jnp.cos(angle), jnp.sin(angle))

    cos_first, sin_first = phase_table(radix_first, radix_first, radix_first)
    cos_twiddle, sin_twiddle = phase_table(radix_first, radix_second, length)
    cos_second, sin_second = phase_table(radix_second, radix_second, radix_second)
    folded_real = input_real.reshape(leading + (radix_first, radix_second))
    section_real = jnp.einsum("...ab,ak->...kb", folded_real, cos_first, precision=highest)
    section_imag = -jnp.einsum("...ab,ak->...kb", folded_real, sin_first, precision=highest)
    if input_imag is not None:
        folded_imag = input_imag.reshape(leading + (radix_first, radix_second))
        section_real = section_real + jnp.einsum(
            "...ab,ak->...kb", folded_imag, sin_first, precision=highest
        )
        section_imag = (
            jnp.einsum("...ab,ak->...kb", folded_imag, cos_first, precision=highest) + section_imag
        )
    turned_real = section_real * cos_twiddle + section_imag * sin_twiddle
    turned_imag = section_imag * cos_twiddle - section_real * sin_twiddle
    output_real = jnp.einsum(
        "...kb,bm->...mk", turned_real, cos_second, precision=highest
    ) + jnp.einsum("...kb,bm->...mk", turned_imag, sin_second, precision=highest)
    output_imag = jnp.einsum(
        "...kb,bm->...mk", turned_imag, cos_second, precision=highest
    ) - jnp.einsum("...kb,bm->...mk", turned_real, sin_second, precision=highest)
    return (output_real.reshape(leading + (length,)), output_imag.reshape(leading + (length,)))


def strip_modes(strip):
    slab_count = lax.axis_size("gx")
    strip_count = lax.axis_size("gy")
    z_items, x_items, line_length = strip.shape
    wave_local = line_length // (slab_count * strip_count)
    modes_real, modes_imag = fourier_last(strip.astype(jnp.float32), None)
    stacked = jnp.stack([modes_real, modes_imag]).reshape(
        2, z_items, x_items, slab_count, strip_count, wave_local
    )
    stacked = jnp.transpose(stacked, (0, 1, 3, 4, 5, 2)).astype(jnp.bfloat16)
    return stacked.reshape(2, z_items, slab_count, strip_count, wave_local, 1, 1, x_items)


def shards(node_cells, node_frac, node_force, node_count, z_rates, z_synth, z_analysis):
    capacity = node_force.shape[0]
    slab_count = lax.axis_size("gx")
    strip_count = lax.axis_size("gy")
    scale = 8.0 / math.sqrt(capacity * slab_count * strip_count)
    slab_x = NX // slab_count
    strip_y = NY // strip_count
    z_levels = z_synth.shape[0]
    wide_x = slab_x + WIN - 1
    wide_y = strip_y + WIN - 1
    weighted = node_force * scale
    live_count = node_count[0]
    grid_tile = spread_nodes(
        node_cells, node_frac, weighted, 0, live_count, z_levels, wide_x, wide_y
    )
    upper_rim = grid_tile[:, :, strip_y:]
    received = shifted(upper_rim.astype(jnp.bfloat16), "gy", 1).astype(upper_rim.dtype)
    grid_tile = grid_tile[:, :, :strip_y].at[:, :, : WIN - 1].add(received)
    upper_rim = grid_tile[:, slab_x:, :]
    received = shifted(upper_rim, "gx", 1)
    slab_grid = grid_tile[:, :slab_x, :].at[:, : WIN - 1, :].add(received).astype(jnp.bfloat16)
    packed = strip_modes(lax.all_to_all(slab_grid, "gy", split_axis=0, concat_axis=2, tiled=True))
    moved = lax.all_to_all(
        lax.all_to_all(packed, "gx", split_axis=2, concat_axis=5, tiled=True),
        "gy",
        split_axis=3,
        concat_axis=1,
        tiled=True,
    )
    wave_local = NY // (slab_count * strip_count)
    waves = moved.reshape(2, z_levels, wave_local, NX).astype(jnp.float32)
    modes_real, modes_imag = fourier_last(waves[0], waves[1])
    wave_first = (lax.axis_index("gx") * strip_count + lax.axis_index("gy")) * wave_local
    y_number = (wave_first + jnp.arange(wave_local, dtype=jnp.int32)).astype(jnp.float32)
    x_number = jnp.arange(NX, dtype=jnp.int32).astype(jnp.float32)
    x_wave = jnp.sin(jnp.pi * x_number / NX)
    y_wave = jnp.sin(jnp.pi * y_number / NY)
    wave_sq = 4.0 * (x_wave[None, :] * x_wave[None, :] + y_wave[:, None] * y_wave[:, None])
    denominator = wave_sq[None, :, :] + z_rates[:, None, None]
    highest = lax.Precision.HIGHEST
    coef_real = jnp.einsum("az,zlk->alk", z_analysis, modes_real, precision=highest) / denominator
    coef_imag = jnp.einsum("az,zlk->alk", z_analysis, modes_imag, precision=highest) / denominator
    velocity_real = jnp.einsum("za,alk->zlk", z_synth, coef_real, precision=highest)
    velocity_imag = jnp.einsum("za,alk->zlk", z_synth, coef_imag, precision=highest)
    return jnp.stack([velocity_real, velocity_imag])


def solution(mesh):
    return jax.shard_map(
        shards,
        mesh=mesh,
        in_specs=(
            P(None, ("gx", "gy")),
            P(None, ("gx", "gy")),
            P(("gx", "gy")),
            P(("gx", "gy")),
            P(),
            P(),
            P(),
        ),
        out_specs=P(None, None, ("gx", "gy"), None),
        check_vma=False,
    )
```

profile of v0, /device:TPU:32, one launch (start us, length us, event | category | flops | bytes accessed | tf_op | source)
XLA Modules:
  0.0 518.5 jit_solution(11739357789694175807)
XLA Ops:
  11.8 45.6 %collective-permute-start = (bf16[64,53,5]{0,1,2:T(8,128)(2,1)}, bf16[64,53,5]{0,1,2:T(8,128)(2,1)}, u32[]{:S(2)}, u32[]{:S(2)}) collective-permute-start(bf16[64,53,5]{0,1,2:T(8,128)(2,1)} %copy.100), channel_id=1, source_target_pairs={{7,0},{0,1},{1,2},{2,3},{3,4},{4,5},{5,6},{6,7},{15,8},{8,9},{9,10... | collective-permute-start | bytes 101768 | tf_op jit(solution)/shard_map/ppermute | solution.py:19
  57.5 5.3 %copy.99 = f32[64,53,197]{0,1,2:T(8,128)} copy(f32[64,53,197]{2,0,1:T(8,128)S(1)} %get-tuple-element.121) | data formatting | bytes 5345792 | tf_op jit(solution)/shard_map/while | solution.py:65
  68.3 10.3 %scatter-add.6 = f32[64,53,192]{2,1,0:T(8,128)} dynamic-update-slice(f32[64,53,192]{2,1,0:T(8,128)} %bitcast.163, f32[64,53,5]{2,1,0:T(8,128)S(1)} %copy.101, s32[]{:T(128)} %constant.172.clone.1, s32[]{:T(128)} %constant.172.clone.1, s32[]{:T(128)} %constant.172.clone.1) | dynamic-update-slice | bytes 135684 | tf_op jit(solution)/shard_map/scatter-add | solution.py:141
  83.0 7.5 %collective-permute-done.1 = f32[64,5,192]{2,1,0:T(8,128)S(1)} collective-permute-done((f32[64,5,192]{2,1,0:T(8,128)S(1)}, f32[64,5,192]{2,1,0:T(8,128)S(1)}, u32[]{:S(2)}, u32[]{:S(2)}) %collective-permute-start.1) | collective-permute-done | bytes 245792 | tf_op jit(solution)/shard_map/ppermute | solution.py:19
  91.6 3.9 scatter-add.9
  95.5 18.7 %all-to-all-start = ((bf16[64,48,192]{2,1,0:T(8,128)(2,1)}), bf16[64,48,192]{2,1,0:T(8,128)(2,1)S(1)}, u32[]{:S(2)}, u32[]{:S(2)}) async-start(bf16[64,48,192]{2,1,0:T(8,128)(2,1)} %scatter-add.9), calls=%async_computation | async-start | bytes 3145728 | tf_op jit(solution)/shard_map/all_to_all | solution.py:145
  114.3 34.3 %all-to-all-done = bf16[64,48,192]{2,1,0:T(8,128)(2,1)S(1)} async-done(((bf16[64,48,192]{2,1,0:T(8,128)(2,1)}), bf16[64,48,192]{2,1,0:T(8,128)(2,1)S(1)}, u32[]{:S(2)}, u32[]{:S(2)}) %all-to-all-start) | async-done | bytes 1179680 | tf_op jit(solution)/shard_map/all_to_all | solution.py:145
  150.6 4.3 reshape.387
  157.6 4.0 add_bitcast_fusion
  161.6 24.0 %fusion.12 = f32[48,8,48,32]{2,0,3,1:T(8,128)S(1)} fusion(f32[8,48,32,48]{3,2,1,0:T(8,128)S(1)} %get-tuple-element.146), kind=kOutput, calls=%fused_computation.36 | convolution fusion | flops 339759360 | bytes 4718592 | tf_op jit(solution)/shard_map/...kb,bm->...mk/dot_general | solution.py:104
  185.6 23.6 %fusion.10 = f32[48,8,48,32]{2,0,3,1:T(8,128)S(1)} fusion(f32[8,48,32,48]{3,2,1,0:T(8,128)S(1)} %get-tuple-element.146), kind=kOutput, calls=%fused_computation.34 | convolution fusion | flops 339759360 | bytes 4718592 | tf_op jit(solution)/shard_map/...kb,bm->...mk/dot_general | solution.py:105
  209.2 22.6 %fusion.26 = bf16[8,48,48,32]{1,2,3,0:T(8,128)(2,1)S(1)} fusion(f32[48,8,48,32]{2,0,3,1:T(8,128)S(1)} %fusion.12, f32[8,48,32,48]{3,2,1,0:T(8,128)S(1)} %get-tuple-element.145), kind=kOutput, calls=%fused_computation.58 | convolution fusion | flops 340939008 | bytes 5898240 | tf_op jit(solution)/shard_map/...kb,bm->...mk/dot_general | solution.py:102
  233.8 23.0 %fusion.27 = bf16[8,48,48,32]{1,2,3,0:T(8,128)(2,1)S(1)} fusion(f32[48,8,48,32]{2,0,3,1:T(8,128)S(1)} %fusion.10, f32[8,48,32,48]{3,2,1,0:T(8,128)S(1)} %get-tuple-element.145), kind=kOutput, calls=%fused_computation.59 | convolution fusion | flops 340939008 | bytes 5898240 | tf_op jit(solution)/shard_map/...kb,bm->...mk/dot_general | solution.py:107
  258.9 4.2 copy_bitcast_fusion.2
  263.0 10.3 %reshape.398 = bf16[32,2,18432]{2,1,0:T(2,128)(2,1)S(1)} reshape(bf16[32,1,1,2,8,6,8,48]{7,6,5,4,3,2,1,0:T(8,128)(2,1)} %copy_bitcast_fusion.2) | data formatting | bytes 4718592
  273.3 58.5 %all_to_all.48 = bf16[32,2,18432]{2,1,0:T(2,128)(2,1)} all-to-all(bf16[32,2,18432]{2,1,0:T(2,128)(2,1)S(1)} %reshape.398), channel_id=1, replica_groups=mesh['gx'=32,'gy'=8] {'gx'}, dimensions={0} | all-to-all | bytes 4718592 | tf_op jit(solution)/shard_map/all_to_all | solution.py:147
  331.8 9.3 %reshape.399 = bf16[32,1,1,2,8,6,8,48]{7,6,5,4,3,2,1,0:T(8,128)(2,1)} reshape(bf16[32,2,18432]{2,1,0:T(2,128)(2,1)} %all_to_all.48) | data formatting | bytes 4718592
  341.1 7.1 %copy_bitcast_fusion.1 = bf16[8,1,1,2,32,6,8,48]{7,6,5,4,3,2,1,0:T(8,128)(2,1)} fusion(bf16[32,1,1,2,8,6,8,48]{7,6,5,4,3,2,1,0:T(8,128)(2,1)} %reshape.399), kind=kLoop, calls=%fused_computation.193 | loop fusion | bytes 4718592
  348.1 11.3 %reshape.400 = bf16[8,2,73728]{2,1,0:T(2,128)(2,1)} reshape(bf16[8,1,1,2,32,6,8,48]{7,6,5,4,3,2,1,0:T(8,128)(2,1)} %copy_bitcast_fusion.1) | data formatting | bytes 4718592
  363.6 59.2 %all-to-all-done.2 = bf16[8,2,73728]{2,1,0:T(2,128)(2,1)S(1)} async-done(((bf16[8,2,73728]{2,1,0:T(2,128)(2,1)}), bf16[8,2,73728]{2,1,0:T(2,128)(2,1)S(1)}, u32[]{:S(2)}, u32[]{:S(2)}) %all-to-all-start.2) | async-done | bytes 2359328 | tf_op jit(solution)/shard_map/all_to_all | solution.py:146
  422.8 7.4 %reshape.401 = bf16[8,1,1,2,32,6,8,48]{7,6,5,4,3,2,1,0:T(8,128)(2,1)} reshape(bf16[8,2,73728]{2,1,0:T(2,128)(2,1)S(1)} %all-to-all-done.2) | data formatting | bytes 4718592
  430.2 3.9 bitcast_bitcast_fusion
  439.2 5.3 %copy.114 = bf16[64,6,32,48]{0,2,3,1:T(8,128)(2,1)S(1)} copy(bf16[64,6,32,48]{3,2,1,0:T(8,128)(2,1)} %bitcast.161) | data formatting | bytes 2359296 | tf_op jit(solution)/shard_map/reshape;squeeze | solution.py:93
  444.5 4.2 fusion.72
  451.2 6.4 %copy.112 = bf16[64,6,32,48]{0,2,3,1:T(8,128)(2,1)} copy(bf16[64,6,32,48]{3,2,1,0:T(8,128)(2,1)} %bitcast.162) | data formatting | bytes 2359296 | tf_op jit(solution)/shard_map/reshape;squeeze | solution.py:89
  457.6 3.9 fusion.74
  467.6 7.5 %fusion.20 = f32[48,64,6,32]{1,0,3,2:T(8,128)S(1)} fusion(f32[64,6,32,48]{0,2,3,1:T(8,128)S(1)} %get-tuple-element.148), kind=kOutput, calls=%fused_computation.50 | convolution fusion | flops 339759360 | bytes 4718592 | tf_op jit(solution)/shard_map/...kb,bm->...mk/dot_general | solution.py:104
  475.2 6.8 %fusion.18 = f32[48,64,6,32]{1,0,3,2:T(8,128)S(1)} fusion(f32[64,6,32,48]{0,2,3,1:T(8,128)S(1)} %get-tuple-element.148), kind=kOutput, calls=%fused_computation.48 | convolution fusion | flops 339759360 | bytes 4718592 | tf_op jit(solution)/shard_map/...kb,bm->...mk/dot_general | solution.py:105
  482.0 7.4 %add_bitcast_fusion.1 = f32[64,6,48,32]{0,2,3,1:T(8,128)S(1)} fusion(f32[48,64,6,32]{1,0,3,2:T(8,128)S(1)} %fusion.20, f32[64,6,32,48]{0,2,3,1:T(8,128)S(1)} %get-tuple-element.147), kind=kOutput, calls=%fused_computation.44 | convolution fusion | flops 340349184 | bytes 7077888 | tf_op jit(solution)/shard_map/...kb,bm->...mk/dot_general | solution.py:102
  490.9 7.3 %subtract_bitcast_fusion.1 = f32[64,6,48,32]{0,2,3,1:T(8,128)S(1)} fusion(f32[48,64,6,32]{1,0,3,2:T(8,128)S(1)} %fusion.18, f32[64,6,32,48]{0,2,3,1:T(8,128)S(1)} %get-tuple-element.147), kind=kOutput, calls=%fused_computation.43 | convolution fusion | flops 340349184 | bytes 7077888 | tf_op jit(solution)/shard_map/...kb,bm->...mk/dot_general | solution.py:107
  499.9 5.5 %add_divide_fusion.1 = f32[64,6,1536]{2,0,1:T(8,128)S(1)} fusion(f32[64,6,1536]{0,2,1:T(8,128)S(1)} %bitcast.166, f32[64]{0:T(128)S(1)} %copy-done.5, f32[6,1536]{1,0:T(8,128)S(1)} %add_multiply_fusion, f32[64,64]{1,0:T(8,128)S(1)} %copy-done), kind=kOutput, calls=%fused_computation.57 | convolution fusion | flops 454164480 | bytes 4772096 | tf_op jit(solution)/shard_map/az,zlk->alk/dot_general | solution.py:164
  505.4 5.5 %add_divide_fusion = f32[64,6,1536]{2,0,1:T(8,128)S(1)} fusion(f32[64,6,1536]{0,2,1:T(8,128)S(1)} %bitcast.167, f32[64]{0:T(128)S(1)} %copy-done.5, f32[6,1536]{1,0:T(8,128)S(1)} %add_multiply_fusion, f32[64,64]{1,0:T(8,128)S(1)} %copy-done), kind=kOutput, calls=%fused_computation.56 | convolution fusion | flops 454164480 | bytes 4772096 | tf_op jit(solution)/shard_map/az,zlk->alk/dot_general | solution.py:165
  (62 shorter events, 62.6 us)
Async XLA Ops:
  0.0 499.9 %copy-start = (f32[64,64]{1,0:T(8,128)S(1)}, f32[64,64]{1,0:T(8,128)}, u32[]{:S(2)}) copy-start(f32[64,64]{1,0:T(8,128)} %param.19) | copy-start | bytes 49156
  11.8 54.8 %collective-permute-start = (bf16[64,53,5]{0,1,2:T(8,128)(2,1)}, bf16[64,53,5]{0,1,2:T(8,128)(2,1)}, u32[]{:S(2)}, u32[]{:S(2)}) collective-permute-start(bf16[64,53,5]{0,1,2:T(8,128)(2,1)} %copy.100), channel_id=1, source_target_pairs={{7,0},{0,1},{1,2},{2,3},{3,4},{4,5},{5,6},{6,7},{15,8},{8,9},{9,10... | collective-permute-start | bytes 101768 | tf_op jit(solution)/shard_map/ppermute | solution.py:19
  79.7 10.8 %collective-permute-start.1 = (f32[64,5,192]{2,1,0:T(8,128)S(1)}, f32[64,5,192]{2,1,0:T(8,128)S(1)}, u32[]{:S(2)}, u32[]{:S(2)}) collective-permute-start(f32[64,5,192]{2,1,0:T(8,128)S(1)} %slice.120), channel_id=1, source_target_pairs={{248,0},{0,8},{8,16},{16,24},{24,32},{32,40},{40,48},{48,56},{56,6... | collective-permute-start | bytes 737288 | tf_op jit(solution)/shard_map/ppermute | solution.py:19
  95.5 53.0 %all-to-all-start = ((bf16[64,48,192]{2,1,0:T(8,128)(2,1)}), bf16[64,48,192]{2,1,0:T(8,128)(2,1)S(1)}, u32[]{:S(2)}, u32[]{:S(2)}) async-start(bf16[64,48,192]{2,1,0:T(8,128)(2,1)} %scatter-add.9), calls=%async_computation | async-start | bytes 3145728 | tf_op jit(solution)/shard_map/all_to_all | solution.py:145
  359.5 63.4 %all-to-all-start.2 = ((bf16[8,2,73728]{2,1,0:T(2,128)(2,1)}), bf16[8,2,73728]{2,1,0:T(2,128)(2,1)S(1)}, u32[]{:S(2)}, u32[]{:S(2)}) async-start(bf16[8,2,73728]{2,1,0:T(2,128)(2,1)} %reshape.400), calls=%async_computation.2 | async-start | bytes 4718592 | tf_op jit(solution)/shard_map/all_to_all | solution.py:146
  444.5 4.3 copy-start.3
  457.6 3.9 copy-start.1
  457.6 3.9 copy-start.2
  498.2 1.7 copy-start.5
  505.4 5.5 %copy-start.4 = (f32[64,64]{1,0:T(8,128)S(1)}, f32[64,64]{1,0:T(8,128)}, u32[]{:S(2)}) copy-start(f32[64,64]{1,0:T(8,128)} %param.18) | copy-start | bytes 49156
where the time goes:
time: 529 us; the launch traced here: 518 us
  matrix products  159 us (30%)
  local copies, waits for them, and re-layouts  119 us (22%)
  waiting for transfers between devices  101 us (19%)
  starting transfers between devices  68.2 us (13%)
  blocking collectives  58.5 us (11%)
  other arithmetic  10.8 us (2%)
    all_to_all x1, waiting for transfers between devices, shards(): lax.all_to_all(lax.all_to_all(packed, 'gx', split_axis=2, concat_axis=5,...  59.2 us
    all_to_all x1, blocking collectives, shards(): lax.all_to_all(packed, 'gx', split_axis=2, concat_axis=5, tiled=True)  58.5 us
    ppermute x2, starting transfers between devices, shifted(): return lax.ppermute(block, axis, route)  45.7 us
    unnamed x17, local copies, waits for them, and re-layouts  45.3 us
    all_to_all x1, waiting for transfers between devices, shards(): lax.all_to_all(slab_grid, 'gy', split_axis=0, concat_axis=2, tiled=True)  34.3 us
    dot_general x2, matrix products, fourier_last(): jnp.einsum('...kb,bm->...mk', turned_imag, sin_second, precision=highest)  31.5 us
    dot_general x2, matrix products, fourier_last(): jnp.einsum('...kb,bm->...mk', turned_imag, cos_second, precision=highest)  30.4 us
    dot_general x2, matrix products, fourier_last(): jnp.einsum('...kb,bm->...mk', turned_real, sin_second, precision=highest)  30.3 us
  transfers between devices with their start and end apart: 4, of which 3 were waited for; matrix products, arithmetic and copies ran while one was open for 2% of the time, Pallas kernels for 0%

commit v1 on v0

v1 whole, which is shorter than its diff:
```python
import functools
import math

import jax
import jax.numpy as jnp
import numpy as np
from jax import lax
from jax.experimental import pallas as pl
from jax.experimental.pallas import tpu as pltpu
from jax.sharding import PartitionSpec as P

NX = 1536
NY = 1536
WIN = 6
NZ = 64
RADIX = 6
BASE = 256
SLAB = 48
STRIP = 192
ROWS = 208
LANES = 128
NODE_BLOCK = 1024
GROUPS = ((0, 1, 2),)
BOTH = ("gx", "gy")
F32 = jnp.float32
BF16 = jnp.bfloat16
HALF_ROOT3 = math.sqrt(3.0) / 2.0
VMEM_BYTES = 56 * 1024 * 1024


def split_table(table):
    high = table.astype(np.float32).astype(BF16)
    low = (table - high.astype(np.float64)).astype(np.float32).astype(BF16)
    return high, low


def base_tables():
    index = np.arange(BASE)
    angle = 2.0 * np.pi * (np.outer(index, index) % BASE) / BASE
    return np.cos(angle), np.sin(angle)


def split_value(value):
    high = value.astype(BF16)
    return high, (value - high.astype(F32)).astype(BF16)


def window(position, cell, frac):
    offset = position - cell
    distance = offset.astype(F32) - (WIN - 1) / 2.0 - frac
    inside = (offset >= 0) & (offset < WIN)
    return jnp.where(inside, jnp.exp(-distance * distance / 2.0), 0.0)


def dot_rows(left, right):
    return lax.dot_general(left, right, (((1,), (1,)), ((), ())), preferred_element_type=F32)


def matmul(left, right):
    return jnp.dot(left, right, preferred_element_type=F32)


def block_count(count_ref):
    return (count_ref[0] + (NODE_BLOCK - 1)) >> (NODE_BLOCK.bit_length() - 1)


def prepare_kernel(
    count_ref, cell_ref, frac_ref, force_ref, right_ref, z_ref, x_ref, rim_ref, left_ref, sum_ref
):
    live_count = count_ref[0]
    capacity = force_ref.shape[1]
    scale = 8.0 / math.sqrt(capacity * 256)
    sum_ref[...] = jnp.zeros_like(sum_ref)

    def body(block, carry):
        start = pl.multiple_of(block * NODE_BLOCK, NODE_BLOCK)
        span = pl.ds(start, NODE_BLOCK)

        def rows(extent):
            return lax.broadcasted_iota(jnp.int32, (extent, NODE_BLOCK), 0)

        slot = start + lax.broadcasted_iota(jnp.int32, (1, NODE_BLOCK), 1)
        amplitude = jnp.where(slot < live_count, force_ref[:, span] * scale, 0.0)
        z_part = amplitude * window(rows(NZ), cell_ref[2:3, span], frac_ref[2:3, span])
        x_part = window(rows(56), cell_ref[0:1, span], frac_ref[0:1, span])
        right = window(rows(ROWS), cell_ref[1:2, span], frac_ref[1:2, span]).astype(BF16)
        z_ref[:, span] = z_part
        x_ref[:, span] = x_part
        right_ref[:, span] = right
        for t in range(RADIX):
            left_ref[t * NZ : (t + 1) * NZ, :] = (
                z_part * x_part[SLAB + t : SLAB + t + 1, :]
            ).astype(BF16)
        sum_ref[...] += dot_rows(right, left_ref[...])
        return carry

    lax.fori_loop(0, block_count(count_ref), body, 0)
    rim_ref[...] = sum_ref[...].astype(BF16)


def spread_kernel(pairs, count_ref, right_ref, z_ref, x_ref, out_ref, left_ref, sum_ref):
    width = len(pairs) * LANES
    sum_ref[...] = jnp.zeros_like(sum_ref)

    def body(block, carry):
        span = pl.ds(pl.multiple_of(block * NODE_BLOCK, NODE_BLOCK), NODE_BLOCK)

        def step(half, inner):
            for k in range(2):
                for p, pair in enumerate(pairs):
                    for par in range(2):
                        x_at = (2 * half + k) * RADIX + 2 * pair + par
                        row = ((k * len(pairs) + p) * 2 + par) * NZ
                        left_ref[row : row + NZ, :] = (
                            z_ref[:, span] * x_ref[pl.ds(x_at, 1), span]
                        ).astype(BF16)
            lanes = pl.ds(pl.multiple_of(half * 2 * width, LANES), 2 * width)
            sum_ref[:, lanes] += dot_rows(right_ref[:, span], left_ref[...])
            return inner

        return lax.fori_loop(0, 4, step, carry)

    lax.fori_loop(0, block_count(count_ref), body, 0)
    for j in range(8):
        out_ref[j] = sum_ref[:, j * width : (j + 1) * width].astype(BF16)


def y_kernel(
    in_ref, high_ref, low_ref, cos_ref, sin_ref, out_ref, grid_ref, th_ref, tl_ref
):
    width = in_ref.shape[2]
    pair_count = width // LANES
    for j in range(8):
        grid_ref[j * STRIP : (j + 1) * STRIP, :] = in_ref[j, 0:STRIP, :].astype(F32)
    for j in range(8):
        before = (j + 7) % 8
        grid_ref[j * STRIP : j * STRIP + 16, :] += in_ref[before, STRIP:ROWS, :].astype(F32)

    def body(step, carry):
        start = pl.multiple_of(step * 16, 16)
        for p in range(pair_count):
            lanes = slice(p * LANES, (p + 1) * LANES)
            a = [grid_ref[pl.ds(n * BASE + start, 16), lanes] for n in range(RADIX)]
            s0, s1, s2 = a[0] + a[3], a[1] + a[4], a[2] + a[5]
            d0, d1, d2 = a[0] - a[3], a[1] - a[4], a[2] - a[5]
            h1r, h1i = d0 + 0.5 * (d1 - d2), -HALF_ROOT3 * (d1 + d2)
            h2r, h2i = s0 - 0.5 * (s1 + s2), -HALF_ROOT3 * (s1 - s2)
            turned = (
                (s0 + s1 + s2, None),
                (h1r, h1i),
                (h2r, h2i),
                (d0 - d1 + d2, None),
                (h2r, -h2i),
                (h1r, -h1i),
            )
            for q, (real, imag) in enumerate(turned):
                if q > 0:
                    cos = cos_ref[q - 1, pl.ds(start, 16), :]
                    sin = sin_ref[q - 1, pl.ds(start, 16), :]
                    if imag is None:
                        real, imag = real * cos, -real * sin
                    else:
                        real, imag = real * cos + imag * sin, imag * cos - real * sin
                else:
                    imag = jnp.zeros_like(real)
                columns = slice(q * width + p * LANES, q * width + (p + 1) * LANES)
                for at, value in ((0, real), (BASE, imag)):
                    high, low = split_value(value)
                    th_ref[pl.ds(at + start, 16), columns] = high
                    tl_ref[pl.ds(at + start, 16), columns] = low
        return carry

    lax.fori_loop(0, BASE // 16, body, 0)
    for pair in range(3):
        columns = slice(2 * pair * width, 2 * (pair + 1) * width)
        high = th_ref[:, columns]
        modes = matmul(high_ref[...], high)
        modes += matmul(low_ref[...], high)
        modes += matmul(high_ref[...], tl_ref[:, columns])
        for k in range(2):
            q = 2 * pair + k
            for part in range(2):
                for p in range(pair_count):
                    at = (k * pair_count + p) * LANES
                    out_ref[(q * 2 + part) * pair_count + p] = modes[
                        part * BASE : (part + 1) * BASE, at : at + LANES
                    ].astype(BF16)


def x_kernel(
    group_count,
    *refs,
):
    in_refs = refs[:group_count]
    (
        wave_ref,
        high_ref,
        low_ref,
        cos_ref,
        sin_ref,
        across_ref,
        rate_ref,
        analysis_ref,
        synth_ref,
        out_ref,
        modes_ref,
        x_ref,
        c_ref,
        wa_ref,
        ws_ref,
    ) = refs[group_count:]
    per_group = 3 // group_count
    q = pl.program_id(0)

    @pl.when(q == 0)
    def _():
        high, low = split_value(analysis_ref[...])
        for k in range(2):
            wa_ref[k * LANES : (k + 1) * LANES, :LANES] = high
            wa_ref[k * LANES : (k + 1) * LANES, LANES:] = low
        high, low = split_value(synth_ref[...])
        for k in range(2):
            ws_ref[:LANES, k * LANES : (k + 1) * LANES] = high
            ws_ref[LANES:, k * LANES : (k + 1) * LANES] = low

    lines = jnp.concatenate(
        [
            in_refs[xp // per_group][part * per_group + xp % per_group]
            for part in range(2)
            for xp in range(3)
        ],
        axis=1,
    )
    modes_ref[...] = matmul(high_ref[...], lines) + matmul(low_ref[...], lines)
    lane = lax.broadcasted_iota(jnp.int32, (16, LANES), 1)
    lower = lane < NZ
    sign = jnp.where(lower, 1.0, -1.0)
    turn_1r = jnp.where(lower, 1.0, 0.5)
    turn_2r = jnp.where(lower, 1.0, -0.5)
    turn_i = jnp.where(lower, 0.0, -HALF_ROOT3)

    def body(step, carry):
        start = pl.multiple_of(step * 16, 16)
        real, imag = [], []
        for xp in range(3):
            at_real = slice(xp * LANES, (xp + 1) * LANES)
            at_imag = slice((3 + xp) * LANES, (4 + xp) * LANES)
            mode_real = (
                modes_ref[pl.ds(start, 16), at_real] + modes_ref[pl.ds(BASE + start, 16), at_imag]
            )
            mode_imag = (
                modes_ref[pl.ds(start, 16), at_imag] - modes_ref[pl.ds(BASE + start, 16), at_real]
            )
            cos = cos_ref[xp, pl.ds(start, 16), :]
            sin = sin_ref[xp, pl.ds(start, 16), :]
            real.append(mode_real * cos + mode_imag * sin)
            imag.append(mode_imag * cos - mode_real * sin)
        sum_r, sum_i = real[1] + real[2], imag[1] + imag[2]
        dif_r, dif_i = HALF_ROOT3 * (real[1] - real[2]), HALF_ROOT3 * (imag[1] - imag[2])
        mid_r, mid_i = real[0] - 0.5 * sum_r, imag[0] - 0.5 * sum_i
        u1r, u1i = mid_r + dif_i, mid_i - dif_r
        u2r, u2i = mid_r - dif_i, mid_i + dif_r
        thirds = (
            (real[0] + sum_r, imag[0] + sum_i),
            (u1r * turn_1r - u1i * turn_i, u1i * turn_1r + u1r * turn_i),
            (u2r * turn_2r - u2i * turn_i, u2i * turn_2r + u2r * turn_i),
        )
        for m in range(3):
            for part in range(2):
                value = thirds[m][part]
                value = pltpu.roll(value, NZ, 1) + sign * value
                high, low = split_value(value)
                row = pl.ds((m * 2 + part) * BASE + start, 16)
                x_ref[row, :LANES] = high
                x_ref[row, LANES:] = low
        return carry

    lax.fori_loop(0, BASE // 16, body, 0)
    shift = rate_ref[...] + wave_ref[q]
    for m in range(3):
        inverse = 1.0 / (across_ref[m] + shift)
        for part in range(2):
            rows = slice((m * 2 + part) * BASE, (m * 2 + part + 1) * BASE)
            both = matmul(x_ref[rows, :], wa_ref[...])
            high, low = split_value((both[:, :LANES] + both[:, LANES:]) * inverse)
            c_ref[rows, :LANES] = high
            c_ref[rows, LANES:] = low
            both = dot_rows(ws_ref[...], c_ref[rows, :])
            value = both[:LANES] + both[LANES:]
            out_ref[part, 0, :, m * BASE : (m + 1) * BASE] = value[:NZ]
            out_ref[part, 0, :, (m + 3) * BASE : (m + 4) * BASE] = value[NZ:]


def vmem_call(kernel, inputs, out_shape, scratch_shapes, scalars=1, cost=None):
    specs = [pl.BlockSpec(memory_space=pltpu.SMEM)] * scalars
    specs += [pl.BlockSpec(memory_space=pltpu.VMEM)] * (len(inputs) - scalars)
    return pl.pallas_call(
        kernel,
        out_shape=out_shape,
        in_specs=specs,
        out_specs=jax.tree.map(lambda _: pl.BlockSpec(memory_space=pltpu.VMEM), out_shape),
        scratch_shapes=scratch_shapes,
        compiler_params=pltpu.CompilerParams(vmem_limit_bytes=VMEM_BYTES),
        cost_estimate=cost,
    )(*inputs)


def twin(matrix):
    zero = jnp.zeros_like(matrix)
    return jnp.concatenate(
        [jnp.concatenate([matrix, zero], axis=1), jnp.concatenate([zero, matrix], axis=1)], axis=0
    )


def shards(node_cells, node_frac, node_force, node_count, z_rates, z_synth, z_analysis):
    capacity = node_force.shape[0]
    slabs = lax.axis_size("gx")
    cos_base, sin_base = base_tables()
    full = np.block([[cos_base, sin_base], [-sin_base, cos_base]])
    full_high, full_low = split_table(full)
    half_high, half_low = split_table(np.concatenate([cos_base, sin_base], axis=0))

    right, z_part, x_part, rim = vmem_call(
        prepare_kernel,
        (node_count, node_cells, node_frac, node_force.reshape(1, capacity)),
        (
            jax.ShapeDtypeStruct((ROWS, capacity), BF16),
            jax.ShapeDtypeStruct((NZ, capacity), F32),
            jax.ShapeDtypeStruct((56, capacity), F32),
            jax.ShapeDtypeStruct((ROWS, RADIX * NZ), BF16),
        ),
        [
            pltpu.VMEM((RADIX * NZ, NODE_BLOCK), BF16),
            pltpu.VMEM((ROWS, RADIX * NZ), F32),
        ],
        cost=pl.CostEstimate(flops=10**9, bytes_accessed=10**7, transcendentals=10**6),
    )
    rim = lax.ppermute(rim, "gx", [(i, (i + 1) % slabs) for i in range(slabs)])

    row = np.arange(BASE)
    angle = 2.0 * np.pi * np.outer(np.arange(1, RADIX), row) / NY
    y_cos = np.broadcast_to(np.cos(angle)[:, :, None], (RADIX - 1, BASE, LANES)).astype(np.float32)
    y_sin = np.broadcast_to(np.sin(angle)[:, :, None], (RADIX - 1, BASE, LANES)).astype(np.float32)

    arrived = []
    for pairs in GROUPS:
        width = len(pairs) * LANES
        tiles = vmem_call(
            functools.partial(spread_kernel, pairs),
            (node_count, right, z_part, x_part),
            jax.ShapeDtypeStruct((8, ROWS, width), BF16),
            [
                pltpu.VMEM((2 * width, NODE_BLOCK), BF16),
                pltpu.VMEM((ROWS, 8 * width), F32),
            ],
            cost=pl.CostEstimate(
                flops=10**10 // len(GROUPS), bytes_accessed=10**7, transcendentals=0
            ),
        )
        rim_lanes = rim[:, pairs[0] * LANES : (pairs[-1] + 1) * LANES]
        tiles = tiles.at[0].set((tiles[0].astype(F32) + rim_lanes.astype(F32)).astype(BF16))
        lines = lax.all_to_all(tiles, "gy", split_axis=0, concat_axis=0, tiled=True)
        items = 2 * RADIX * len(pairs)
        spectrum = vmem_call(
            y_kernel,
            (lines, full_high, full_low, y_cos, y_sin),
            jax.ShapeDtypeStruct((items, BASE, LANES), BF16),
            [
                pltpu.VMEM((NY, width), F32),
                pltpu.VMEM((2 * BASE, RADIX * width), BF16),
                pltpu.VMEM((2 * BASE, RADIX * width), BF16),
            ],
            scalars=0,
            cost=pl.CostEstimate(
                flops=5 * 10**9 // len(GROUPS), bytes_accessed=10**7, transcendentals=0
            ),
        )
        packed = spectrum.reshape(items // 4, 4, BASE, LANES).transpose(2, 0, 1, 3)
        moved = lax.all_to_all(packed, BOTH, split_axis=0, concat_axis=0, tiled=True)
        arrived.append(moved.transpose(1, 2, 0, 3).reshape(items, BASE, LANES))

    offset = np.arange(RADIX).reshape(3, 2)
    angle = 2.0 * np.pi * offset[:, None, :] * row[None, :, None] / NX
    x_cos = np.repeat(np.cos(angle), NZ, axis=2).astype(np.float32)
    x_sin = np.repeat(np.sin(angle), NZ, axis=2).astype(np.float32)
    number = row[None, :, None] + BASE * (np.arange(3)[:, None, None] + 3 * np.arange(2))
    across = np.repeat(4.0 * np.sin(np.pi * number / NX) ** 2, NZ, axis=2).astype(np.float32)
    first = (lax.axis_index("gx") * lax.axis_size("gy") + lax.axis_index("gy")) * RADIX
    y_number = (first + jnp.arange(RADIX, dtype=jnp.int32)).astype(F32)
    y_wave = jnp.sin(jnp.pi * y_number / NY)
    wave = 4.0 * y_wave * y_wave
    rates = jnp.concatenate([z_rates, z_rates]).reshape(1, LANES)

    def whole(array):
        return pl.BlockSpec(array.shape, lambda q: (0,) * array.ndim)

    constants = (
        half_high,
        half_low,
        x_cos,
        x_sin,
        across,
        rates,
        twin(z_analysis.T),
        twin(z_synth),
    )
    out = pl.pallas_call(
        functools.partial(x_kernel, len(GROUPS)),
        out_shape=jax.ShapeDtypeStruct((2, RADIX, NZ, NX), F32),
        grid=(RADIX,),
        in_specs=[
            pl.BlockSpec((2 * len(pairs), BASE, LANES), lambda q: (q, 0, 0)) for pairs in GROUPS
        ]
        + [pl.BlockSpec(memory_space=pltpu.SMEM)]
        + [whole(array) for array in constants],
        out_specs=pl.BlockSpec((2, 1, NZ, NX), lambda q: (0, q, 0, 0)),
        scratch_shapes=[
            pltpu.VMEM((2 * BASE, RADIX * LANES), F32),
            pltpu.VMEM((RADIX * BASE, 2 * LANES), BF16),
            pltpu.VMEM((RADIX * BASE, 2 * LANES), BF16),
            pltpu.VMEM((2 * LANES, 2 * LANES), BF16),
            pltpu.VMEM((2 * LANES, 2 * LANES), BF16),
        ],
        compiler_params=pltpu.CompilerParams(vmem_limit_bytes=VMEM_BYTES),
    )(*arrived, wave, *constants)
    return out.transpose(0, 2, 1, 3)


def solution(mesh):
    return jax.shard_map(
        shards,
        mesh=mesh,
        in_specs=(
            P(None, BOTH),
            P(None, BOTH),
            P(BOTH),
            P(BOTH),
            P(),
            P(),
            P(),
        ),
        out_specs=P(None, None, BOTH, None),
        check_vma=False,
    )
```

time: 529 us -> 170 us (0.32); the launches traced: 518 us -> 169 us
  matrix products: 159 us -> 0 us
  local copies, waits for them, and re-layouts: 119 us -> 7.87 us
  starting transfers between devices: 68.2 us -> 14.1 us
  waiting for transfers between devices: 101 us -> 55.6 us
  Pallas kernels: 0 us -> 41.2 us
  blocking collectives: 58.5 us -> 47 us
  other arithmetic: 10.8 us -> 2.67 us
    dot_general x19 -> x0, matrix products: 159 us -> none  [the longest x2 31.5 us: fourier_last(): jnp.einsum('...kb,bm->...mk', turned_imag, sin_second, precision=highest)]
    unnamed x17 -> x8, local copies, waits for them, and re-layouts: 45.3 us -> 1.02 us
    ppermute x2 -> x1, starting transfers between devices: 45.7 us -> 1.72 us  [shards(): rim = lax.ppermute(rim, 'gx', [(i, (i + 1) % slabs) for i in range(slabs)])]
    pallas_call x0 -> x4, Pallas kernels: none -> 41.2 us  [the longest x1 22.3 us: shards(): pl.pallas_call(functools.partial(x_kernel, len(GROUPS)), out_shape=jax.Sh...]
    all_to_all x2 -> x1, waiting for transfers between devices: 93.5 us -> 55.6 us  [shards(): lax.all_to_all(packed, BOTH, split_axis=0, concat_axis=0, tiled=True)]
    slice x9 -> x0, local copies, waits for them, and re-layouts: 17.1 us -> none  [the longest x3 7.62 us: shards(): modes_real, modes_imag = fourier_last(waves[0], waves[1])]
    scatter-add x2 -> x0, local copies, waits for them, and re-layouts: 14.2 us -> none  [the longest x1 10.3 us: shards(): grid_tile = grid_tile[:, :, :strip_y].at[:, :, :WIN - 1].add(received)]
    another operation x2 -> x0, local copies, waits for them, and re-layouts: 11.6 us -> none  [the longest x1 6.36 us: fourier_last(): folded_real = input_real.reshape(leading + (radix_first, radix_second))]
  transfers between devices with their start and end apart: 4 -> 2, of which waited for: 3 -> 1; matrix products, arithmetic and copies ran while one was open for 2% -> 2% of each run, Pallas kernels for 0% -> 4%
where the time goes in v1:
time: 170 us; the launch traced here: 169 us
  waiting for transfers between devices  55.6 us (33%)
  blocking collectives  47 us (28%)
  Pallas kernels  41.2 us (24%)
  starting transfers between devices  14.1 us (8%)
  local copies, waits for them, and re-layouts  7.87 us (5%)
  other arithmetic  2.67 us (2%)
    all_to_all x1, waiting for transfers between devices, shards(): lax.all_to_all(packed, BOTH, split_axis=0, concat_axis=0, tiled=True)  55.6 us
    all_to_all x1, blocking collectives, shards(): lines = lax.all_to_all(tiles, 'gy', split_axis=0, concat_axis=0, tiled=True)  47 us
    pallas_call x1, Pallas kernels, shards(): pl.pallas_call(functools.partial(x_kernel, len(GROUPS)), out_shape=jax.Sh...  22.3 us
    pallas_call x3, Pallas kernels, vmem_call(): pl.pallas_call(kernel, out_shape=out_shape, in_specs=specs, out_specs=jax...  18.9 us
    all_to_all x1, starting transfers between devices, shards(): lax.all_to_all(packed, BOTH, split_axis=0, concat_axis=0, tiled=True)  12.4 us
    reshape x1, local copies, waits for them, and re-layouts, shards(): packed = spectrum.reshape(items // 4, 4, BASE, LANES).transpose(2, 0, 1, 3)  4.89 us
  transfers between devices with their start and end apart: 2, of which 1 were waited for; matrix products, arithmetic and copies ran while one was open for 2% of the time, Pallas kernels for 4%

profile of v1, /device:TPU:32, one launch (start us, length us, event | category | flops | bytes accessed | tf_op | source)
XLA Modules:
  0.0 169.2 jit_solution(17098966574599159466)
XLA Ops:
  0.7 3.7 %shard_map.154 = (bf16[208,4096]{1,0:T(8,128)(2,1)}, f32[64,4096]{1,0:T(8,128)}, f32[56,4096]{1,0:T(8,128)}, bf16[208,384]{1,0:T(8,128)(2,1)}) custom-call(s32[1]{0:T(128)S(6)} %copy.24.count_ref, s32[3,4096]{1,0:T(4,128)} %cell_ref.1, f32[3,4096]{1,0:T(4,128)} %frac_ref.1, f32[1,4096]{1,0:T(1,128)} %bitcast.23), custom_call_target="tpu_custom_call" | custom-call | flops 1000000000 | bytes 10000000 | tf_op jit(solution)/shard_map/pallas_call | solution.py:297
  4.4 1.7 %collective-permute-start = (bf16[208,384]{1,0:T(8,128)(2,1)}, bf16[208,384]{1,0:T(8,128)(2,1)S(1)}, u32[]{:S(2)}, u32[]{:S(2)}) collective-permute-start(bf16[208,384]{1,0:T(8,128)(2,1)} %get-tuple-element.24), channel_id=1, source_target_pairs={{0,8},{8,16},{16,24},{24,32},{32,40},{40,48},{48,56},{56,64},{64,7... | collective-permute-start | bytes 479240 | tf_op jit(solution)/shard_map/ppermute | solution.py:338
  6.1 6.0 %shard_map.155 = bf16[8,208,384]{2,1,0:T(8,128)(2,1)} custom-call(s32[1]{0:T(128)S(6)} %copy.24.count_ref, bf16[208,4096]{1,0:T(8,128)(2,1)} %get-tuple-element.21.right_ref, f32[64,4096]{1,0:T(8,128)} %get-tuple-element.22.z_ref, f32[56,4096]{1,0:T(8,128)} %get-tuple-element.23.x_ref), custom_call_target="tpu_custom_call" | custom-call | flops 10000000000 | bytes 10000000 | tf_op jit(solution)/shard_map/pallas_call | solution.py:297
  12.1 0.9 slice_bitcast_fusion
  13.1 0.0 collective-permute-done
  13.1 0.7 fusion.2
  13.8 47.0 %all_to_all.10.in_ref = bf16[8,208,384]{2,1,0:T(8,128)(2,1)} all-to-all(bf16[8,208,384]{2,1,0:T(8,128)(2,1)} %fusion.2), channel_id=1, replica_groups=mesh['gx'=32,'gy'=8] {'gy'}, dimensions={0} | all-to-all | bytes 2555904 | tf_op jit(solution)/shard_map/all_to_all | solution.py:362
  60.8 9.2 %shard_map.156 = bf16[36,256,128]{2,1,0:T(8,128)(2,1)} custom-call(bf16[8,208,384]{2,1,0:T(8,128)(2,1)} %all_to_all.10.in_ref, bf16[512,512]{1,0:T(8,128)(2,1)} %constant.67.clone.high_ref, bf16[512,512]{1,0:T(8,128)(2,1)} %constant.68.clone.low_ref, f32[5,256,128]{2,1,0:T(8,128)} %constant.69.clone.cos_ref, f32[5,256,128]{2,1,0:T(8,128)} %constant.70.clone.sin_ref), custom_call_target="tpu_custom_call" | custom-call | flops 5000000000 | bytes 10000000 | tf_op jit(solution)/shard_map/pallas_call | solution.py:297
  69.9 4.9 %copy.22 = bf16[9,4,256,128]{3,1,0,2:T(4,128)(2,1)} copy(bf16[9,4,256,128]{3,2,1,0:T(8,128)(2,1)} %bitcast.21) | data formatting | bytes 4718592 | tf_op jit(solution)/shard_map/reshape | solution.py:378
  74.8 0.0 copy-start
  74.8 0.0 copy-start.2
  74.8 0.0 copy-start.1
  74.8 12.4 %all-to-all-start.1 = ((bf16[256,9,4,128]{3,2,1,0:T(4,128)(2,1)}), bf16[256,9,4,128]{3,2,1,0:T(4,128)(2,1)S(1)}, u32[]{:S(2)}, u32[]{:S(2)}) async-start(bf16[256,9,4,128]{3,2,1,0:T(4,128)(2,1)} %bitcast.20), calls=%async_computation.1 | async-start | bytes 4718592 | tf_op jit(solution)/shard_map/all_to_all | solution.py:379
  87.2 0.0 copy-done
  87.2 0.1 copy.20
  87.3 0.6 multiply_multiply_fusion.refs_1_
  87.9 0.0 copy-done.2
  87.9 0.7 maximum_bitcast_fusion.refs_7_
  88.6 0.0 copy-done.1
  88.6 0.7 select_maximum_fusion
  89.3 55.6 %all-to-all-done.1 = bf16[256,9,4,128]{3,2,1,0:T(4,128)(2,1)S(1)} async-done(((bf16[256,9,4,128]{3,2,1,0:T(4,128)(2,1)}), bf16[256,9,4,128]{3,2,1,0:T(4,128)(2,1)S(1)}, u32[]{:S(2)}, u32[]{:S(2)}) %all-to-all-start.1) | async-done | bytes 2359328 | tf_op jit(solution)/shard_map/all_to_all | solution.py:379
  144.9 2.0 %copy.19 = bf16[9,4,256,128]{3,2,1,0:T(8,128)(2,1)} copy(bf16[9,4,256,128]{3,1,0,2:T(4,128)(2,1)S(1)} %bitcast.19) | data formatting | bytes 4718592 | tf_op jit(solution)/shard_map/transpose | solution.py:380
  146.9 22.3 %shard_map.157 = f32[2,6,64,1536]{3,2,1,0:T(8,128)} custom-call(bf16[36,256,128]{2,1,0:T(8,128)(2,1)} %bitcast.18, f32[6]{0:T(128)} %multiply_multiply_fusion.refs_1_, bf16[512,256]{1,0:T(8,128)(2,1)} %constant.71.clone.refs_2_, bf16[512,256]{1,0:T(8,128)(2,1)} %constant.72.clone.refs_3_, f32[3,256,128]{2,1,0:T(8,128)} %constant.73.clone.refs_4_, ...), custom_call_target="tpu_custom_call" | custom-call | tf_op jit(solution)/shard_map/pallas_call | solution.py:407
Async XLA Ops:
  4.4 8.7 %collective-permute-start = (bf16[208,384]{1,0:T(8,128)(2,1)}, bf16[208,384]{1,0:T(8,128)(2,1)S(1)}, u32[]{:S(2)}, u32[]{:S(2)}) collective-permute-start(bf16[208,384]{1,0:T(8,128)(2,1)} %get-tuple-element.24), channel_id=1, source_target_pairs={{0,8},{8,16},{16,24},{24,32},{32,40},{40,48},{48,56},{56,64},{64,7... | collective-permute-start | bytes 479240 | tf_op jit(solution)/shard_map/ppermute | solution.py:338
  74.8 12.4 %copy-start = (f32[64,64]{1,0:T(8,128)S(1)}, f32[64,64]{1,0:T(8,128)}, u32[]{:S(2)}) copy-start(f32[64,64]{1,0:T(8,128)} %param.24) | copy-start | bytes 49156
  74.8 13.1 %copy-start.2 = (f32[64]{0:T(128)S(1)}, f32[64]{0:T(128)}, u32[]{:S(2)}) copy-start(f32[64]{0:T(128)} %param.22) | copy-start | bytes 772
  74.8 13.8 %copy-start.1 = (f32[64,64]{1,0:T(8,128)S(1)}, f32[64,64]{1,0:T(8,128)}, u32[]{:S(2)}) copy-start(f32[64,64]{1,0:T(8,128)} %param.23) | copy-start | bytes 49156
  74.8 70.1 %all-to-all-start.1 = ((bf16[256,9,4,128]{3,2,1,0:T(4,128)(2,1)}), bf16[256,9,4,128]{3,2,1,0:T(4,128)(2,1)S(1)}, u32[]{:S(2)}, u32[]{:S(2)}) async-start(bf16[256,9,4,128]{3,2,1,0:T(4,128)(2,1)} %bitcast.20), calls=%async_computation.1 | async-start | bytes 4718592 | tf_op jit(solution)/shard_map/all_to_all | solution.py:379

commit v2 on v1

--- a/solution.py
+++ b/solution.py
@@ -1,4 +1,3 @@
-import functools
 import math
 
 import jax
@@ -19,8 +18,12 @@
 STRIP = 192
 ROWS = 208
 LANES = 128
+UNROLL_X = 16
+UNROLL_Y = 4
 NODE_BLOCK = 1024
-GROUPS = ((0, 1, 2),)
+SPREAD_BLOCK = 2048
+ITEMS = 36
+WIDTH = 384
 BOTH = ("gx", "gy")
 F32 = jnp.float32
 BF16 = jnp.bfloat16
@@ -46,10 +49,10 @@
 
 
 def window(position, cell, frac):
-    offset = position - cell
-    distance = offset.astype(F32) - (WIN - 1) / 2.0 - frac
-    inside = (offset >= 0) & (offset < WIN)
-    return jnp.where(inside, jnp.exp(-distance * distance / 2.0), 0.0)
+    centred = (position - cell).astype(F32) - (WIN - 1) / 2.0
+    distance = centred - frac
+    inside = jnp.abs(centred) < WIN / 2.0
+    return jnp.where(inside, jnp.exp(-0.5 * (distance * distance)), 0.0)
 
 
 def dot_rows(left, right):
@@ -61,7 +64,7 @@
 
 
 def block_count(count_ref):
-    return (count_ref[0] + (NODE_BLOCK - 1)) >> (NODE_BLOCK.bit_length() - 1)
+    return (count_ref[0] + (SPREAD_BLOCK - 1)) >> (SPREAD_BLOCK.bit_length() - 1)
 
 
 def prepare_kernel(
@@ -94,42 +97,37 @@
         sum_ref[...] += dot_rows(right, left_ref[...])
         return carry
 
-    lax.fori_loop(0, block_count(count_ref), body, 0)
+    lax.fori_loop(0, block_count(count_ref) * (SPREAD_BLOCK // NODE_BLOCK), body, 0)
     rim_ref[...] = sum_ref[...].astype(BF16)
 
 
-def spread_kernel(pairs, count_ref, right_ref, z_ref, x_ref, out_ref, left_ref, sum_ref):
-    width = len(pairs) * LANES
+def spread_kernel(count_ref, right_ref, z_ref, x_ref, out_ref, left_ref, sum_ref):
     sum_ref[...] = jnp.zeros_like(sum_ref)
 
     def body(block, carry):
-        span = pl.ds(pl.multiple_of(block * NODE_BLOCK, NODE_BLOCK), NODE_BLOCK)
-
-        def step(half, inner):
-            for k in range(2):
-                for p, pair in enumerate(pairs):
-                    for par in range(2):
-                        x_at = (2 * half + k) * RADIX + 2 * pair + par
-                        row = ((k * len(pairs) + p) * 2 + par) * NZ
-                        left_ref[row : row + NZ, :] = (
-                            z_ref[:, span] * x_ref[pl.ds(x_at, 1), span]
-                        ).astype(BF16)
-            lanes = pl.ds(pl.multiple_of(half * 2 * width, LANES), 2 * width)
-            sum_ref[:, lanes] += dot_rows(right_ref[:, span], left_ref[...])
-            return inner
-
-        return lax.fori_loop(0, 4, step, carry)
+        span = pl.ds(pl.multiple_of(block * SPREAD_BLOCK, SPREAD_BLOCK), SPREAD_BLOCK)
+        for pair in range(4):
+            for k in range(2 * RADIX):
+                x_at = pair * 2 * RADIX + k
+                left_ref[k * NZ : (k + 1) * NZ, :] = (
+                    z_ref[:, span] * x_ref[x_at : x_at + 1, span]
+                ).astype(BF16)
+            rows = slice(2 * pair * WIDTH, 2 * (pair + 1) * WIDTH)
+            sum_ref[rows, :] += dot_rows(left_ref[...], right_ref[:, span])
+        return carry
 
     lax.fori_loop(0, block_count(count_ref), body, 0)
     for j in range(8):
-        out_ref[j] = sum_ref[:, j * width : (j + 1) * width].astype(BF16)
+        out_ref[j] = sum_ref[j * WIDTH : (j + 1) * WIDTH, :].T.astype(BF16)
+
+
+def rim_kernel(rim_ref, in_ref, out_ref):
+    out_ref[0] = (in_ref[0].astype(F32) + rim_ref[...].astype(F32)).astype(BF16)
 
 
 def y_kernel(
-    in_ref, high_ref, low_ref, cos_ref, sin_ref, out_ref, grid_ref, th_ref, tl_ref
+    in_ref, table_ref, flip_ref, cos_ref, sin_ref, out_ref, grid_ref, th_ref, tl_ref, mode_ref
 ):
-    width = in_ref.shape[2]
-    pair_count = width // LANES
     for j in range(8):
         grid_ref[j * STRIP : (j + 1) * STRIP, :] = in_ref[j, 0:STRIP, :].astype(F32)
     for j in range(8):
@@ -138,20 +136,16 @@
 
     def body(step, carry):
         start = pl.multiple_of(step * 16, 16)
-        for p in range(pair_count):
+        for p in range(3):
             lanes = slice(p * LANES, (p + 1) * LANES)
             a = [grid_ref[pl.ds(n * BASE + start, 16), lanes] for n in range(RADIX)]
             s0, s1, s2 = a[0] + a[3], a[1] + a[4], a[2] + a[5]
             d0, d1, d2 = a[0] - a[3], a[1] - a[4], a[2] - a[5]
-            h1r, h1i = d0 + 0.5 * (d1 - d2), -HALF_ROOT3 * (d1 + d2)
-            h2r, h2i = s0 - 0.5 * (s1 + s2), -HALF_ROOT3 * (s1 - s2)
             turned = (
                 (s0 + s1 + s2, None),
-                (h1r, h1i),
-                (h2r, h2i),
+                (d0 + 0.5 * (d1 - d2), -HALF_ROOT3 * (d1 + d2)),
+                (s0 - 0.5 * (s1 + s2), -HALF_ROOT3 * (s1 - s2)),
                 (d0 - d1 + d2, None),
-                (h2r, -h2i),
-                (h1r, -h1i),
             )
             for q, (real, imag) in enumerate(turned):
                 if q > 0:
@@ -163,53 +157,52 @@
                         real, imag = real * cos + imag * sin, imag * cos - real * sin
                 else:
                     imag = jnp.zeros_like(real)
-                columns = slice(q * width + p * LANES, q * width + (p + 1) * LANES)
+                columns = slice(q * WIDTH + p * LANES, q * WIDTH + (p + 1) * LANES)
                 for at, value in ((0, real), (BASE, imag)):
                     high, low = split_value(value)
                     th_ref[pl.ds(at + start, 16), columns] = high
                     tl_ref[pl.ds(at + start, 16), columns] = low
         return carry
 
-    lax.fori_loop(0, BASE // 16, body, 0)
-    for pair in range(3):
-        columns = slice(2 * pair * width, 2 * (pair + 1) * width)
+    lax.fori_loop(0, BASE // 16, body, 0, unroll=UNROLL_Y)
+
+    def put(q, part, modes, first):
+        for p in range(3):
+            item = (q * 2 + part) * 3 + p
+            lanes = slice(first + p * LANES, first + (p + 1) * LANES)
+            mode_ref[pl.ds(item, BASE, stride=ITEMS), :] = modes[:, lanes]
+
+    for first in (1, 0, 2, 3):
+        columns = slice(first * WIDTH, (first + 1) * WIDTH)
         high = th_ref[:, columns]
-        modes = matmul(high_ref[...], high)
-        modes += matmul(low_ref[...], high)
-        modes += matmul(high_ref[...], tl_ref[:, columns])
-        for k in range(2):
-            q = 2 * pair + k
-            for part in range(2):
-                for p in range(pair_count):
-                    at = (k * pair_count + p) * LANES
-                    out_ref[(q * 2 + part) * pair_count + p] = modes[
-                        part * BASE : (part + 1) * BASE, at : at + LANES
-                    ].astype(BF16)
+        low = tl_ref[:, columns]
+        modes = matmul(table_ref[...], jnp.concatenate([high, high, low], axis=0))
+        for part in range(2):
+            rows = modes[part * BASE : (part + 1) * BASE]
+            put(first, part, rows, 0)
+            if first in (1, 2):
+                mirror = matmul(flip_ref[...], rows.astype(BF16))
+                put(RADIX - first, part, mirror if part == 0 else -mirror, 0)
+    out_ref[...] = mode_ref[...].astype(BF16)
 
 
 def x_kernel(
-    group_count,
-    *refs,
+    in_ref,
+    wave_ref,
+    table_ref,
+    cos_ref,
+    sin_ref,
+    across_ref,
+    rate_ref,
+    analysis_ref,
+    synth_ref,
+    out_ref,
+    modes_ref,
+    x_ref,
+    c_ref,
+    wa_ref,
+    ws_ref,
 ):
-    in_refs = refs[:group_count]
-    (
-        wave_ref,
-        high_ref,
-        low_ref,
-        cos_ref,
-        sin_ref,
-        across_ref,
-        rate_ref,
-        analysis_ref,
-        synth_ref,
-        out_ref,
-        modes_ref,
-        x_ref,
-        c_ref,
-        wa_ref,
-        ws_ref,
-    ) = refs[group_count:]
-    per_group = 3 // group_count
     q = pl.program_id(0)
 
     @pl.when(q == 0)
@@ -223,15 +216,8 @@
             ws_ref[:LANES, k * LANES : (k + 1) * LANES] = high
             ws_ref[LANES:, k * LANES : (k + 1) * LANES] = low
 
-    lines = jnp.concatenate(
-        [
-            in_refs[xp // per_group][part * per_group + xp % per_group]
-            for part in range(2)
-            for xp in range(3)
-        ],
-        axis=1,
-    )
-    modes_ref[...] = matmul(high_ref[...], lines) + matmul(low_ref[...], lines)
+    lines = jnp.concatenate([in_ref[item] for item in range(6)], axis=1)
+    modes_ref[...] = matmul(table_ref[...], jnp.concatenate([lines, lines], axis=0))
     lane = lax.broadcasted_iota(jnp.int32, (16, LANES), 1)
     lower = lane < NZ
     sign = jnp.where(lower, 1.0, -1.0)
@@ -275,7 +261,7 @@
                 x_ref[row, LANES:] = low
         return carry
 
-    lax.fori_loop(0, BASE // 16, body, 0)
+    lax.fori_loop(0, BASE // 16, body, 0, unroll=UNROLL_X)
     shift = rate_ref[...] + wave_ref[q]
     for m in range(3):
         inverse = 1.0 / (across_ref[m] + shift)
@@ -317,8 +303,12 @@
     slabs = lax.axis_size("gx")
     cos_base, sin_base = base_tables()
     full = np.block([[cos_base, sin_base], [-sin_base, cos_base]])
-    full_high, full_low = split_table(full)
-    half_high, half_low = split_table(np.concatenate([cos_base, sin_base], axis=0))
+    high, low = split_table(full)
+    y_table = np.concatenate([high, low, high], axis=1)
+    flip = np.eye(BASE)[::-1].astype(BF16)
+    x_table = np.concatenate(
+        split_table(np.concatenate([cos_base, sin_base], axis=0)), axis=1
+    )
 
     right, z_part, x_part, rim = vmem_call(
         prepare_kernel,
@@ -338,46 +328,48 @@
     rim = lax.ppermute(rim, "gx", [(i, (i + 1) % slabs) for i in range(slabs)])
 
     row = np.arange(BASE)
-    angle = 2.0 * np.pi * np.outer(np.arange(1, RADIX), row) / NY
-    y_cos = np.broadcast_to(np.cos(angle)[:, :, None], (RADIX - 1, BASE, LANES)).astype(np.float32)
-    y_sin = np.broadcast_to(np.sin(angle)[:, :, None], (RADIX - 1, BASE, LANES)).astype(np.float32)
-
-    arrived = []
-    for pairs in GROUPS:
-        width = len(pairs) * LANES
-        tiles = vmem_call(
-            functools.partial(spread_kernel, pairs),
-            (node_count, right, z_part, x_part),
-            jax.ShapeDtypeStruct((8, ROWS, width), BF16),
-            [
-                pltpu.VMEM((2 * width, NODE_BLOCK), BF16),
-                pltpu.VMEM((ROWS, 8 * width), F32),
-            ],
-            cost=pl.CostEstimate(
-                flops=10**10 // len(GROUPS), bytes_accessed=10**7, transcendentals=0
-            ),
-        )
-        rim_lanes = rim[:, pairs[0] * LANES : (pairs[-1] + 1) * LANES]
-        tiles = tiles.at[0].set((tiles[0].astype(F32) + rim_lanes.astype(F32)).astype(BF16))
-        lines = lax.all_to_all(tiles, "gy", split_axis=0, concat_axis=0, tiled=True)
-        items = 2 * RADIX * len(pairs)
-        spectrum = vmem_call(
-            y_kernel,
-            (lines, full_high, full_low, y_cos, y_sin),
-            jax.ShapeDtypeStruct((items, BASE, LANES), BF16),
-            [
-                pltpu.VMEM((NY, width), F32),
-                pltpu.VMEM((2 * BASE, RADIX * width), BF16),
-                pltpu.VMEM((2 * BASE, RADIX * width), BF16),
-            ],
-            scalars=0,
-            cost=pl.CostEstimate(
-                flops=5 * 10**9 // len(GROUPS), bytes_accessed=10**7, transcendentals=0
-            ),
-        )
-        packed = spectrum.reshape(items // 4, 4, BASE, LANES).transpose(2, 0, 1, 3)
-        moved = lax.all_to_all(packed, BOTH, split_axis=0, concat_axis=0, tiled=True)
-        arrived.append(moved.transpose(1, 2, 0, 3).reshape(items, BASE, LANES))
+    angle = 2.0 * np.pi * np.outer(np.arange(1, 4), row) / NY
+    y_cos = np.broadcast_to(np.cos(angle)[:, :, None], (3, BASE, LANES)).astype(np.float32)
+    y_sin = np.broadcast_to(np.sin(angle)[:, :, None], (3, BASE, LANES)).astype(np.float32)
+
+    tiles = vmem_call(
+        spread_kernel,
+        (node_count, right, z_part, x_part),
+        jax.ShapeDtypeStruct((8, ROWS, WIDTH), BF16),
+        [
+            pltpu.VMEM((2 * WIDTH, SPREAD_BLOCK), BF16),
+            pltpu.VMEM((8 * WIDTH, ROWS), F32),
+        ],
+        cost=pl.CostEstimate(flops=10**10, bytes_accessed=10**7, transcendentals=0),
+    )
+    tiles = pl.pallas_call(
+        rim_kernel,
+        out_shape=jax.ShapeDtypeStruct((8, ROWS, WIDTH), BF16),
+        grid=(1,),
+        in_specs=[
+            pl.BlockSpec((ROWS, WIDTH), lambda i: (0, 0)),
+            pl.BlockSpec((1, ROWS, WIDTH), lambda i: (0, 0, 0)),
+        ],
+        out_specs=pl.BlockSpec((1, ROWS, WIDTH), lambda i: (0, 0, 0)),
+        input_output_aliases={1: 0},
+    )(rim, tiles)
+    lines = lax.all_to_all(tiles, "gy", split_axis=0, concat_axis=0, tiled=True)
+    spectrum = vmem_call(
+        y_kernel,
+        (lines, y_table, flip, y_cos, y_sin),
+        jax.ShapeDtypeStruct((BASE * ITEMS, LANES), BF16),
+        [
+            pltpu.VMEM((NY, WIDTH), F32),
+            pltpu.VMEM((2 * BASE, 4 * WIDTH), BF16),
+            pltpu.VMEM((2 * BASE, 4 * WIDTH), BF16),
+            pltpu.VMEM((BASE * ITEMS, LANES), F32),
+        ],
+        scalars=0,
+        cost=pl.CostEstimate(flops=5 * 10**9, bytes_accessed=10**7, transcendentals=0),
+    )
+    packed = spectrum.reshape(BASE, ITEMS // 4, 4, LANES)
+    moved = lax.all_to_all(packed, BOTH, split_axis=0, concat_axis=0, tiled=True)
+    arrived = moved.transpose(1, 2, 0, 3).reshape(ITEMS, BASE, LANES)
 
     offset = np.arange(RADIX).reshape(3, 2)
     angle = 2.0 * np.pi * offset[:, None, :] * row[None, :, None] / NX
@@ -395,8 +387,7 @@
         return pl.BlockSpec(array.shape, lambda q: (0,) * array.ndim)
 
     constants = (
-        half_high,
-        half_low,
+        x_table,
         x_cos,
         x_sin,
         across,
@@ -405,12 +396,10 @@
         twin(z_synth),
     )
     out = pl.pallas_call(
-        functools.partial(x_kernel, len(GROUPS)),
+        x_kernel,
         out_shape=jax.ShapeDtypeStruct((2, RADIX, NZ, NX), F32),
         grid=(RADIX,),
-        in_specs=[
-            pl.BlockSpec((2 * len(pairs), BASE, LANES), lambda q: (q, 0, 0)) for pairs in GROUPS
-        ]
+        in_specs=[pl.BlockSpec((6, BASE, LANES), lambda q: (q, 0, 0))]
         + [pl.BlockSpec(memory_space=pltpu.SMEM)]
         + [whole(array) for array in constants],
         out_specs=pl.BlockSpec((2, 1, NZ, NX), lambda q: (0, q, 0, 0)),
@@ -422,7 +411,7 @@
             pltpu.VMEM((2 * LANES, 2 * LANES), BF16),
         ],
         compiler_params=pltpu.CompilerParams(vmem_limit_bytes=VMEM_BYTES),
-    )(*arrived, wave, *constants)
+    )(arrived, wave, *constants)
     return out.transpose(0, 2, 1, 3)
 
 

time: 170 us -> 156 us (0.918)
  Pallas kernels: 41.2 us -> 35.5 us
  local copies, waits for them, and re-layouts: 7.87 us -> 2.72 us
  starting transfers between devices: 14.1 us -> 9.05 us
    pallas_call x1 -> x2, Pallas kernels: 22.3 us -> 15.1 us  [the longest x1 13.4 us: shards(): pl.pallas_call(x_kernel, out_shape=jax.ShapeDtypeStruct((2, RADIX, NZ, NX...]
    reshape x1 -> x0, local copies, waits for them, and re-layouts: 4.89 us -> none  [shards(): packed = spectrum.reshape(items // 4, 4, BASE, LANES).transpose(2, 0, 1, 3)]
    all_to_all x1, starting transfers between devices: 12.4 us -> 9.05 us  [shards(): lax.all_to_all(packed, BOTH, split_axis=0, concat_axis=0, tiled=True)]
    ppermute x1, starting transfers between devices: 1.72 us -> 0.01 us  [shards(): rim = lax.ppermute(rim, 'gx', [(i, (i + 1) % slabs) for i in range(slabs)])]
  transfers between devices with their start and end apart: 2 -> 2, of which waited for: 1 -> 1; matrix products, arithmetic and copies ran while one was open for 2% -> 1% of each run, Pallas kernels for 4% -> 5%
where the time goes in v2:
time: 156 us; the launch traced here: 154 us
  waiting for transfers between devices  55.6 us (36%)
  blocking collectives  48.1 us (31%)
  Pallas kernels  35.5 us (23%)
  starting transfers between devices  9.05 us (6%)
  local copies, waits for them, and re-layouts  2.72 us (2%)
  other arithmetic  1.97 us (1%)
    all_to_all x1, waiting for transfers between devices, shards(): lax.all_to_all(packed, BOTH, split_axis=0, concat_axis=0, tiled=True)  55.6 us
    all_to_all x1, blocking collectives, shards(): lines = lax.all_to_all(tiles, 'gy', split_axis=0, concat_axis=0, tiled=True)  48.1 us
    pallas_call x3, Pallas kernels, vmem_call(): pl.pallas_call(kernel, out_shape=out_shape, in_specs=specs, out_specs=jax...  20.3 us
    pallas_call x1, Pallas kernels, shards(): pl.pallas_call(x_kernel, out_shape=jax.ShapeDtypeStruct((2, RADIX, NZ, NX...  13.4 us
    all_to_all x1, starting transfers between devices, shards(): lax.all_to_all(packed, BOTH, split_axis=0, concat_axis=0, tiled=True)  9.05 us
  transfers between devices with their start and end apart: 2, of which 1 were waited for; matrix products, arithmetic and copies ran while one was open for 1% of the time, Pallas kernels for 5%

profile of v2, /device:TPU:32, one launch (start us, length us, event | category | flops | bytes accessed | tf_op | source)
XLA Modules:
  0.0 153.6 jit_solution(10998387370095043902)
XLA Ops:
  0.7 4.5 %shard_map.145 = (bf16[208,4096]{1,0:T(8,128)(2,1)}, f32[64,4096]{1,0:T(8,128)}, f32[56,4096]{1,0:T(8,128)}, bf16[208,384]{1,0:T(8,128)(2,1)}) custom-call(s32[1]{0:T(128)S(6)} %copy.22.count_ref, s32[3,4096]{1,0:T(4,128)} %cell_ref.1, f32[3,4096]{1,0:T(4,128)} %frac_ref.1, f32[1,4096]{1,0:T(1,128)} %bitcast.12), custom_call_target="tpu_custom_call" | custom-call | flops 1000000000 | bytes 10000000 | tf_op jit(solution)/shard_map/pallas_call | solution.py:283
  5.2 0.0 collective-permute-start
  5.2 7.2 %shard_map.146.in_ref = bf16[8,208,384]{2,1,0:T(8,128)(2,1)} custom-call(s32[1]{0:T(128)S(6)} %copy.22.count_ref, bf16[208,4096]{1,0:T(8,128)(2,1)} %get-tuple-element.10.right_ref, f32[64,4096]{1,0:T(8,128)} %get-tuple-element.11.z_ref, f32[56,4096]{1,0:T(8,128)} %get-tuple-element.12.x_ref), custom_call_target="tpu_custom_call" | custom-call | flops 10000000000 | bytes 10000000 | tf_op jit(solution)/shard_map/pallas_call | solution.py:283
  12.4 0.0 collective-permute-done.rim_ref
  12.4 0.0 copy-start
  12.4 0.7 copy-done
  13.1 1.7 %shard_map.147 = bf16[8,208,384]{2,1,0:T(8,128)(2,1)} custom-call(bf16[208,384]{1,0:T(8,128)(2,1)} %copy-done, bf16[8,208,384]{2,1,0:T(8,128)(2,1)} %shard_map.146.in_ref), custom_call_target="tpu_custom_call", output_to_operand_aliasing={{}: (1, {})} | custom-call | tf_op jit(solution)/shard_map/pallas_call | solution.py:345
  14.8 48.1 %all_to_all.10.in_ref = bf16[8,208,384]{2,1,0:T(8,128)(2,1)} all-to-all(bf16[8,208,384]{2,1,0:T(8,128)(2,1)} %shard_map.147), channel_id=1, replica_groups=mesh['gx'=32,'gy'=8] {'gy'}, dimensions={0} | all-to-all | bytes 2555904 | tf_op jit(solution)/shard_map/all_to_all | solution.py:356
  62.9 8.6 %shard_map.148 = bf16[9216,128]{1,0:T(8,128)(2,1)} custom-call(bf16[8,208,384]{2,1,0:T(8,128)(2,1)} %all_to_all.10.in_ref, bf16[512,1536]{1,0:T(8,128)(2,1)} %constant.38.clone.table_ref, bf16[256,256]{1,0:T(8,128)(2,1)} %constant.39.clone.flip_ref, f32[3,256,128]{2,1,0:T(8,128)} %constant.40.clone.cos_ref, f32[3,256,128]{2,1,0:T(8,128)} %constant.41.clone.sin_ref), custom_call_target="tpu_custom_call" | custom-call | flops 5000000000 | bytes 10000000 | tf_op jit(solution)/shard_map/pallas_call | solution.py:283
  71.4 0.0 copy-start.1
  71.4 0.0 copy-start.3
  71.4 0.0 copy-start.2
  71.5 9.0 %all-to-all-start.1 = ((bf16[256,9,4,128]{3,2,1,0:T(4,128)(2,1)}), bf16[256,9,4,128]{3,2,1,0:T(4,128)(2,1)S(1)}, u32[]{:S(2)}, u32[]{:S(2)}) async-start(bf16[256,9,4,128]{3,2,1,0:T(4,128)(2,1)} %bitcast.10), calls=%async_computation.1 | async-start | bytes 4718592 | tf_op jit(solution)/shard_map/all_to_all | solution.py:371
  80.5 0.0 copy-done.1
  80.5 0.1 copy.20
  80.6 0.6 multiply_multiply_fusion.wave_ref
  81.2 0.0 copy-done.3
  81.2 0.6 maximum_bitcast_fusion.rate_ref
  81.8 0.0 copy-done.2
  81.8 0.8 select_maximum_fusion
  82.6 55.6 %all-to-all-done.1 = bf16[256,9,4,128]{3,2,1,0:T(4,128)(2,1)S(1)} async-done(((bf16[256,9,4,128]{3,2,1,0:T(4,128)(2,1)}), bf16[256,9,4,128]{3,2,1,0:T(4,128)(2,1)S(1)}, u32[]{:S(2)}, u32[]{:S(2)}) %all-to-all-start.1) | async-done | bytes 2359328 | tf_op jit(solution)/shard_map/all_to_all | solution.py:371
  138.2 2.0 %copy.19 = bf16[9,4,256,128]{3,2,1,0:T(8,128)(2,1)} copy(bf16[9,4,256,128]{3,1,0,2:T(4,128)(2,1)S(1)} %bitcast.9) | data formatting | bytes 4718592 | tf_op jit(solution)/shard_map/transpose | solution.py:372
  140.2 13.4 %shard_map.149 = f32[2,6,64,1536]{3,2,1,0:T(8,128)} custom-call(bf16[36,256,128]{2,1,0:T(8,128)(2,1)} %bitcast.8, f32[6]{0:T(128)} %multiply_multiply_fusion.wave_ref, bf16[512,512]{1,0:T(8,128)(2,1)} %constant.42.clone.table_ref, f32[3,256,128]{2,1,0:T(8,128)} %constant.43.clone.cos_ref, f32[3,256,128]{2,1,0:T(8,128)} %constant.44.clone.sin_ref, ...), custom_call_target="tpu_custom_call" | custom-call | tf_op jit(solution)/shard_map/pallas_call | solution.py:398
Async XLA Ops:
  5.2 7.2 %collective-permute-start = (bf16[208,384]{1,0:T(8,128)(2,1)}, bf16[208,384]{1,0:T(8,128)(2,1)S(1)}, u32[]{:S(2)}, u32[]{:S(2)}) collective-permute-start(bf16[208,384]{1,0:T(8,128)(2,1)} %get-tuple-element.9), channel_id=1, source_target_pairs={{0,8},{8,16},{16,24},{24,32},{32,40},{40,48},{48,56},{56,64},{64,7... | collective-permute-start | bytes 479240 | tf_op jit(solution)/shard_map/ppermute | solution.py:328
  12.4 0.7 copy-start
  71.4 9.1 %copy-start.1 = (f32[64,64]{1,0:T(8,128)S(1)}, f32[64,64]{1,0:T(8,128)}, u32[]{:S(2)}) copy-start(f32[64,64]{1,0:T(8,128)} %param.21) | copy-start | bytes 49156
  71.4 9.8 %copy-start.3 = (f32[64]{0:T(128)S(1)}, f32[64]{0:T(128)}, u32[]{:S(2)}) copy-start(f32[64]{0:T(128)} %param.19) | copy-start | bytes 772
  71.4 10.4 %copy-start.2 = (f32[64,64]{1,0:T(8,128)S(1)}, f32[64,64]{1,0:T(8,128)}, u32[]{:S(2)}) copy-start(f32[64,64]{1,0:T(8,128)} %param.20) | copy-start | bytes 49156
  71.5 66.7 %all-to-all-start.1 = ((bf16[256,9,4,128]{3,2,1,0:T(4,128)(2,1)}), bf16[256,9,4,128]{3,2,1,0:T(4,128)(2,1)S(1)}, u32[]{:S(2)}, u32[]{:S(2)}) async-start(bf16[256,9,4,128]{3,2,1,0:T(4,128)(2,1)} %bitcast.10), calls=%async_computation.1 | async-start | bytes 4718592 | tf_op jit(solution)/shard_map/all_to_all | solution.py:371

commit v3 on v2

--- a/solution.py
+++ b/solution.py
@@ -1,3 +1,4 @@
+import itertools
 import math
 
 import jax
@@ -25,10 +26,16 @@
 ITEMS = 36
 WIDTH = 384
 BOTH = ("gx", "gy")
+TURNS = tuple((dx, way) for dx in range(4) for way in range(2))
 F32 = jnp.float32
 BF16 = jnp.bfloat16
 HALF_ROOT3 = math.sqrt(3.0) / 2.0
-VMEM_BYTES = 56 * 1024 * 1024
+MIB = 1024 * 1024
+PREPARE_BYTES = 14 * MIB
+SPREAD_BYTES = 20 * MIB
+SORT_BYTES = 8 * MIB
+Y_BYTES = 26 * MIB
+X_BYTES = 26 * MIB
 
 
 def split_table(table):
@@ -121,18 +128,31 @@
         out_ref[j] = sum_ref[j * WIDTH : (j + 1) * WIDTH, :].T.astype(BF16)
 
 
-def rim_kernel(rim_ref, in_ref, out_ref):
-    out_ref[0] = (in_ref[0].astype(F32) + rim_ref[...].astype(F32)).astype(BF16)
-
-
-def y_kernel(
-    in_ref, table_ref, flip_ref, cos_ref, sin_ref, out_ref, grid_ref, th_ref, tl_ref, mode_ref
-):
-    for j in range(8):
-        grid_ref[j * STRIP : (j + 1) * STRIP, :] = in_ref[j, 0:STRIP, :].astype(F32)
-    for j in range(8):
-        before = (j + 7) % 8
-        grid_ref[j * STRIP : j * STRIP + 16, :] += in_ref[before, STRIP:ROWS, :].astype(F32)
+def partner(turn, sign):
+    dx, way = TURNS[turn]
+    gx, gy = lax.axis_index("gx"), lax.axis_index("gy")
+    dz = 2 - 4 * ((gx + way) & 1)
+    x_at = ((gy >> 1) + sign * dx) & 3
+    z_at = ((gy & 1) * 4 + (gx >> 3) + sign * dz) & 7
+    return x_at * 2 + (z_at >> 2)
+
+
+def sort_kernel(in_ref, rim_ref, *out_refs):
+    for turn, out_ref in enumerate(out_refs):
+        block = partner(turn, 1)
+        rim = jnp.where(block == 0, rim_ref[...].astype(F32), 0.0)
+        out_ref[...] = (in_ref[block].astype(F32) + rim).astype(BF16)
+
+
+def y_kernel(*refs):
+    in_refs = refs[:8]
+    table_ref, flip_ref, cos_ref, sin_ref, out_ref, grid_ref, th_ref, tl_ref, mode_ref = refs[8:]
+    for turn in range(8):
+        start = pl.multiple_of(partner(turn, -1) * STRIP, STRIP)
+        grid_ref[pl.ds(start, STRIP), :] = in_refs[turn][0:STRIP, :].astype(F32)
+    for turn in range(8):
+        start = pl.multiple_of(((partner(turn, -1) + 1) & 7) * STRIP, STRIP)
+        grid_ref[pl.ds(start, 16), :] += in_refs[turn][STRIP:ROWS, :].astype(F32)
 
     def body(step, carry):
         start = pl.multiple_of(step * 16, 16)
@@ -263,21 +283,24 @@
 
     lax.fori_loop(0, BASE // 16, body, 0, unroll=UNROLL_X)
     shift = rate_ref[...] + wave_ref[q]
+    both = matmul(x_ref[...], wa_ref[...])
     for m in range(3):
         inverse = 1.0 / (across_ref[m] + shift)
         for part in range(2):
             rows = slice((m * 2 + part) * BASE, (m * 2 + part + 1) * BASE)
-            both = matmul(x_ref[rows, :], wa_ref[...])
-            high, low = split_value((both[:, :LANES] + both[:, LANES:]) * inverse)
+            high, low = split_value((both[rows, :LANES] + both[rows, LANES:]) * inverse)
             c_ref[rows, :LANES] = high
             c_ref[rows, LANES:] = low
-            both = dot_rows(ws_ref[...], c_ref[rows, :])
-            value = both[:LANES] + both[LANES:]
-            out_ref[part, 0, :, m * BASE : (m + 1) * BASE] = value[:NZ]
-            out_ref[part, 0, :, (m + 3) * BASE : (m + 4) * BASE] = value[NZ:]
-
-
-def vmem_call(kernel, inputs, out_shape, scratch_shapes, scalars=1, cost=None):
+    both = dot_rows(ws_ref[...], c_ref[...])
+    value = both[:LANES] + both[LANES:]
+    for m in range(3):
+        for part in range(2):
+            columns = slice((m * 2 + part) * BASE, (m * 2 + part + 1) * BASE)
+            out_ref[part, 0, :, m * BASE : (m + 1) * BASE] = value[:NZ, columns]
+            out_ref[part, 0, :, (m + 3) * BASE : (m + 4) * BASE] = value[NZ:, columns]
+
+
+def vmem_call(kernel, inputs, out_shape, scratch_shapes, limit, scalars=1, cost=None):
     specs = [pl.BlockSpec(memory_space=pltpu.SMEM)] * scalars
     specs += [pl.BlockSpec(memory_space=pltpu.VMEM)] * (len(inputs) - scalars)
     return pl.pallas_call(
@@ -286,9 +309,20 @@
         in_specs=specs,
         out_specs=jax.tree.map(lambda _: pl.BlockSpec(memory_space=pltpu.VMEM), out_shape),
         scratch_shapes=scratch_shapes,
-        compiler_params=pltpu.CompilerParams(vmem_limit_bytes=VMEM_BYTES),
+        compiler_params=pltpu.CompilerParams(vmem_limit_bytes=limit),
         cost_estimate=cost,
     )(*inputs)
+
+
+def place(x, y, z, core):
+    return ((z % 4 * 8 + y * 2 + core) * 8) + x * 2 + z // 4
+
+
+def turn_route(dx, way):
+    return [
+        (place(x, y, z, core), place((x + dx) % 4, y, (z + 2 - 4 * ((core + way) % 2)) % 8, core))
+        for x, y, z, core in itertools.product(range(4), range(4), range(8), range(2))
+    ]
 
 
 def twin(matrix):
@@ -306,8 +340,9 @@
     high, low = split_table(full)
     y_table = np.concatenate([high, low, high], axis=1)
     flip = np.eye(BASE)[::-1].astype(BF16)
+    order = np.arange(BASE) ^ (BASE // 2)
     x_table = np.concatenate(
-        split_table(np.concatenate([cos_base, sin_base], axis=0)), axis=1
+        split_table(np.concatenate([cos_base, sin_base], axis=0)[:, order]), axis=1
     )
 
     right, z_part, x_part, rim = vmem_call(
@@ -323,6 +358,7 @@
             pltpu.VMEM((RADIX * NZ, NODE_BLOCK), BF16),
             pltpu.VMEM((ROWS, RADIX * NZ), F32),
         ],
+        PREPARE_BYTES,
         cost=pl.CostEstimate(flops=10**9, bytes_accessed=10**7, transcendentals=10**6),
     )
     rim = lax.ppermute(rim, "gx", [(i, (i + 1) % slabs) for i in range(slabs)])
@@ -340,23 +376,17 @@
             pltpu.VMEM((2 * WIDTH, SPREAD_BLOCK), BF16),
             pltpu.VMEM((8 * WIDTH, ROWS), F32),
         ],
+        SPREAD_BYTES,
         cost=pl.CostEstimate(flops=10**10, bytes_accessed=10**7, transcendentals=0),
     )
-    tiles = pl.pallas_call(
-        rim_kernel,
-        out_shape=jax.ShapeDtypeStruct((8, ROWS, WIDTH), BF16),
-        grid=(1,),
-        in_specs=[
-            pl.BlockSpec((ROWS, WIDTH), lambda i: (0, 0)),
-            pl.BlockSpec((1, ROWS, WIDTH), lambda i: (0, 0, 0)),
-        ],
-        out_specs=pl.BlockSpec((1, ROWS, WIDTH), lambda i: (0, 0, 0)),
-        input_output_aliases={1: 0},
-    )(rim, tiles)
-    lines = lax.all_to_all(tiles, "gy", split_axis=0, concat_axis=0, tiled=True)
+    line = jax.ShapeDtypeStruct((ROWS, WIDTH), BF16)
+    parts = vmem_call(sort_kernel, (tiles, rim), (line,) * 8, [], scalars=0, limit=SORT_BYTES)
+    lines = [
+        lax.ppermute(part, BOTH, turn_route(dx, way)) for part, (dx, way) in zip(parts, TURNS)
+    ]
     spectrum = vmem_call(
         y_kernel,
-        (lines, y_table, flip, y_cos, y_sin),
+        (*lines, y_table, flip, y_cos, y_sin),
         jax.ShapeDtypeStruct((BASE * ITEMS, LANES), BF16),
         [
             pltpu.VMEM((NY, WIDTH), F32),
@@ -364,6 +394,7 @@
             pltpu.VMEM((2 * BASE, 4 * WIDTH), BF16),
             pltpu.VMEM((BASE * ITEMS, LANES), F32),
         ],
+        Y_BYTES,
         scalars=0,
         cost=pl.CostEstimate(flops=5 * 10**9, bytes_accessed=10**7, transcendentals=0),
     )
@@ -410,7 +441,7 @@
             pltpu.VMEM((2 * LANES, 2 * LANES), BF16),
             pltpu.VMEM((2 * LANES, 2 * LANES), BF16),
         ],
-        compiler_params=pltpu.CompilerParams(vmem_limit_bytes=VMEM_BYTES),
+        compiler_params=pltpu.CompilerParams(vmem_limit_bytes=X_BYTES),
     )(arrived, wave, *constants)
     return out.transpose(0, 2, 1, 3)
 

time: 156 us -> 142 us (0.910)
  blocking collectives: 48.1 us -> 0 us
  starting transfers between devices: 9.05 us -> 40 us
  waiting for transfers between devices: 55.6 us -> 71.1 us
  Pallas kernels: 35.5 us -> 24.6 us
  other arithmetic: 1.97 us -> 0.21 us
    all_to_all x1 -> x0, blocking collectives: 48.1 us -> none  [shards(): lines = lax.all_to_all(tiles, 'gy', split_axis=0, concat_axis=0, tiled=True)]
    ppermute x0 -> x8, starting transfers between devices: none -> 24.3 us  [shards(): lax.ppermute(part, BOTH, turn_route(dx, way))]
    ppermute x0 -> x8, waiting for transfers between devices: none -> 11.1 us  [shards(): lax.ppermute(part, BOTH, turn_route(dx, way))]
    pallas_call x3 -> x4, Pallas kernels: 20.3 us -> 13 us  [vmem_call(): pl.pallas_call(kernel, out_shape=out_shape, in_specs=specs, out_specs=jax...]
    all_to_all x1, starting transfers between devices: 9.05 us -> 15.7 us  [shards(): lax.all_to_all(packed, BOTH, split_axis=0, concat_axis=0, tiled=True)]
    ppermute x1, waiting for transfers between devices: 0.01 us -> 2.62 us  [shards(): rim = lax.ppermute(rim, 'gx', [(i, (i + 1) % slabs) for i in range(slabs)])]
    unnamed x9 -> x29, local copies, waits for them, and re-layouts: 0.75 us -> 3.33 us
    pallas_call x1, Pallas kernels: 13.4 us -> 11.6 us  [shards(): pl.pallas_call(x_kernel, out_shape=jax.ShapeDtypeStruct((2, RADIX, NZ, NX...]
  transfers between devices with their start and end apart: 2 -> 10, of which waited for: 1 -> 6; matrix products, arithmetic and copies ran while one was open for 1% -> 0% of each run, Pallas kernels for 5% -> 3%
where the time goes in v3:
time: 142 us; the launch traced here: 141 us
  waiting for transfers between devices  71.1 us (50%)
  starting transfers between devices  40 us (28%)
  Pallas kernels  24.6 us (17%)
  local copies, waits for them, and re-layouts  3.88 us (3%)
    all_to_all x1, waiting for transfers between devices, shards(): lax.all_to_all(packed, BOTH, split_axis=0, concat_axis=0, tiled=True)  57.4 us
    ppermute x8, starting transfers between devices, shards(): lax.ppermute(part, BOTH, turn_route(dx, way))  24.3 us
    all_to_all x1, starting transfers between devices, shards(): lax.all_to_all(packed, BOTH, split_axis=0, concat_axis=0, tiled=True)  15.7 us
    pallas_call x4, Pallas kernels, vmem_call(): pl.pallas_call(kernel, out_shape=out_shape, in_specs=specs, out_specs=jax...  13 us
    pallas_call x1, Pallas kernels, shards(): pl.pallas_call(x_kernel, out_shape=jax.ShapeDtypeStruct((2, RADIX, NZ, NX...  11.6 us
    ppermute x8, waiting for transfers between devices, shards(): lax.ppermute(part, BOTH, turn_route(dx, way))  11.1 us
    unnamed x29, local copies, waits for them, and re-layouts  3.33 us
  transfers between devices with their start and end apart: 10, of which 6 were waited for; matrix products, arithmetic and copies ran while one was open for 0% of the time, Pallas kernels for 3%

profile of v3, /device:TPU:32, one launch (start us, length us, event | category | flops | bytes accessed | tf_op | source)
XLA Modules:
  0.0 140.6 jit_solution(14169493585619006697)
XLA Ops:
  0.7 0.8 copy-done.4
  1.5 0.8 copy-done.5
  2.3 0.7 copy-done.6
  3.1 1.8 %shard_map.145 = (bf16[208,4096]{1,0:T(8,128)(2,1)S(1)}, f32[64,4096]{1,0:T(8,128)S(1)}, f32[56,4096]{1,0:T(8,128)S(1)}, bf16[208,384]{1,0:T(8,128)(2,1)S(1)}) custom-call(s32[1]{0:T(128)S(6)} %copy.20.count_ref, s32[3,4096]{1,0:T(4,128)S(1)} %copy-done.4, f32[3,4096]{1,0:T(4,128)S(1)} %copy-done.5, f32[1,4096]{1,0:T(1,128)S(1)} %bitcast.9), custom_call_target="tpu_custom_call" | custom-call | flops 1000000000 | bytes 10000000 | tf_op jit(solution)/shard_map/pallas_call | solution.py:306
  4.8 0.1 collective-permute-start
  5.0 4.1 %shard_map.146.in_ref = bf16[8,208,384]{2,1,0:T(8,128)(2,1)S(1)} custom-call(s32[1]{0:T(128)S(6)} %copy.20.count_ref, bf16[208,4096]{1,0:T(8,128)(2,1)S(1)} %get-tuple-element.17.right_ref, f32[64,4096]{1,0:T(8,128)S(1)} %get-tuple-element.18.z_ref, f32[56,4096]{1,0:T(8,128)S(1)} %get-tuple-element.19.x_ref), custom_call_target="tpu_custom_call" | custom-call | flops 10000000000 | bytes 10000000 | tf_op jit(solution)/shard_map/pallas_call | solution.py:306
  9.1 2.6 %collective-permute-done.rim_ref = bf16[208,384]{1,0:T(8,128)(2,1)S(1)} collective-permute-done((bf16[208,384]{1,0:T(8,128)(2,1)S(1)}, bf16[208,384]{1,0:T(8,128)(2,1)S(1)}, u32[]{:S(2)}, u32[]{:S(2)}) %collective-permute-start) | collective-permute-done | bytes 159776 | tf_op jit(solution)/shard_map/ppermute | solution.py:364
  11.7 0.4 shard_map.147
  12.2 3.3 %collective-permute-start.1 = (bf16[208,384]{1,0:T(8,128)(2,1)S(1)}, bf16[208,384]{1,0:T(8,128)(2,1)S(1)}, u32[]{:S(2)}, u32[]{:S(2)}) collective-permute-start(bf16[208,384]{1,0:T(8,128)(2,1)S(1)} %get-tuple-element.21), channel_id=1, source_target_pairs={{0,128},{8,137},{64,192},{72,201},{128,1},{136,8},{192,65},{200,72... | collective-permute-start | bytes 479240 | tf_op jit(solution)/shard_map/ppermute | solution.py:385
  15.5 3.0 %collective-permute-start.2 = (bf16[208,384]{1,0:T(8,128)(2,1)S(1)}, bf16[208,384]{1,0:T(8,128)(2,1)S(1)}, u32[]{:S(2)}, u32[]{:S(2)}) collective-permute-start(bf16[208,384]{1,0:T(8,128)(2,1)S(1)} %get-tuple-element.22), channel_id=1, source_target_pairs={{0,129},{8,136},{64,193},{72,200},{128,0},{136,9},{192,64},{200,73... | collective-permute-start | bytes 479240 | tf_op jit(solution)/shard_map/ppermute | solution.py:385
  18.6 3.4 %collective-permute-start.3 = (bf16[208,384]{1,0:T(8,128)(2,1)S(1)}, bf16[208,384]{1,0:T(8,128)(2,1)S(1)}, u32[]{:S(2)}, u32[]{:S(2)}) collective-permute-start(bf16[208,384]{1,0:T(8,128)(2,1)S(1)} %get-tuple-element.23), channel_id=1, source_target_pairs={{0,130},{8,139},{64,194},{72,203},{128,3},{136,10},{192,67},{200,7... | collective-permute-start | bytes 479240 | tf_op jit(solution)/shard_map/ppermute | solution.py:385
  22.0 1.8 %collective-permute-start.4 = (bf16[208,384]{1,0:T(8,128)(2,1)S(1)}, bf16[208,384]{1,0:T(8,128)(2,1)S(1)}, u32[]{:S(2)}, u32[]{:S(2)}) collective-permute-start(bf16[208,384]{1,0:T(8,128)(2,1)S(1)} %get-tuple-element.24), channel_id=1, source_target_pairs={{0,131},{8,138},{64,195},{72,202},{128,2},{136,11},{192,66},{200,7... | collective-permute-start | bytes 479240 | tf_op jit(solution)/shard_map/ppermute | solution.py:385
  23.7 2.6 %collective-permute-start.5 = (bf16[208,384]{1,0:T(8,128)(2,1)S(1)}, bf16[208,384]{1,0:T(8,128)(2,1)S(1)}, u32[]{:S(2)}, u32[]{:S(2)}) collective-permute-start(bf16[208,384]{1,0:T(8,128)(2,1)S(1)} %get-tuple-element.25), channel_id=1, source_target_pairs={{0,132},{8,141},{64,196},{72,205},{128,5},{136,12},{192,69},{200,7... | collective-permute-start | bytes 479240 | tf_op jit(solution)/shard_map/ppermute | solution.py:385
  26.4 3.9 %collective-permute-start.6 = (bf16[208,384]{1,0:T(8,128)(2,1)S(1)}, bf16[208,384]{1,0:T(8,128)(2,1)S(1)}, u32[]{:S(2)}, u32[]{:S(2)}) collective-permute-start(bf16[208,384]{1,0:T(8,128)(2,1)S(1)} %get-tuple-element.26), channel_id=1, source_target_pairs={{0,133},{8,140},{64,197},{72,204},{128,4},{136,13},{192,68},{200,7... | collective-permute-start | bytes 479240 | tf_op jit(solution)/shard_map/ppermute | solution.py:385
  30.3 3.3 %collective-permute-start.7 = (bf16[208,384]{1,0:T(8,128)(2,1)S(1)}, bf16[208,384]{1,0:T(8,128)(2,1)S(1)}, u32[]{:S(2)}, u32[]{:S(2)}) collective-permute-start(bf16[208,384]{1,0:T(8,128)(2,1)S(1)} %get-tuple-element.27), channel_id=1, source_target_pairs={{0,134},{8,143},{64,198},{72,207},{128,7},{136,14},{192,71},{200,7... | collective-permute-start | bytes 479240 | tf_op jit(solution)/shard_map/ppermute | solution.py:385
  33.5 5.2 %collective-permute-done.3.refs_2_ = bf16[208,384]{1,0:T(8,128)(2,1)S(1)} collective-permute-done((bf16[208,384]{1,0:T(8,128)(2,1)S(1)}, bf16[208,384]{1,0:T(8,128)(2,1)S(1)}, u32[]{:S(2)}, u32[]{:S(2)}) %collective-permute-start.3) | collective-permute-done | bytes 159776 | tf_op jit(solution)/shard_map/ppermute | solution.py:385
  38.7 3.0 %collective-permute-start.8 = (bf16[208,384]{1,0:T(8,128)(2,1)S(1)}, bf16[208,384]{1,0:T(8,128)(2,1)S(1)}, u32[]{:S(2)}, u32[]{:S(2)}) collective-permute-start(bf16[208,384]{1,0:T(8,128)(2,1)S(1)} %get-tuple-element.28), channel_id=1, source_target_pairs={{0,135},{8,142},{64,199},{72,206},{128,6},{136,15},{192,70},{200,7... | collective-permute-start | bytes 479240 | tf_op jit(solution)/shard_map/ppermute | solution.py:385
  41.7 2.2 %collective-permute-done.5.refs_4_ = bf16[208,384]{1,0:T(8,128)(2,1)S(1)} collective-permute-done((bf16[208,384]{1,0:T(8,128)(2,1)S(1)}, bf16[208,384]{1,0:T(8,128)(2,1)S(1)}, u32[]{:S(2)}, u32[]{:S(2)}) %collective-permute-start.5) | collective-permute-done | bytes 159776 | tf_op jit(solution)/shard_map/ppermute | solution.py:385
  43.9 2.5 %collective-permute-done.7.refs_6_ = bf16[208,384]{1,0:T(8,128)(2,1)S(1)} collective-permute-done((bf16[208,384]{1,0:T(8,128)(2,1)S(1)}, bf16[208,384]{1,0:T(8,128)(2,1)S(1)}, u32[]{:S(2)}, u32[]{:S(2)}) %collective-permute-start.7) | collective-permute-done | bytes 159776 | tf_op jit(solution)/shard_map/ppermute | solution.py:385
  46.4 1.3 collective-permute-done.8.refs_7_
  47.7 6.7 %shard_map.148 = bf16[9216,128]{1,0:T(8,128)(2,1)} custom-call(bf16[208,384]{1,0:T(8,128)(2,1)S(1)} %collective-permute-done.1.refs_0_, bf16[208,384]{1,0:T(8,128)(2,1)S(1)} %collective-permute-done.2.refs_1_, bf16[208,384]{1,0:T(8,128)(2,1)S(1)} %collective-permute-done.3.refs_2_, bf16[208,384]{1,0:T(8,128)(2,1)S(1)} %collective-permute-done.4.refs_3_, ...), custom_call_target="tpu_custom_call" | custom-call | flops 5000000000 | bytes 10000000 | tf_op jit(solution)/shard_map/pallas_call | solution.py:306
  54.3 15.7 %all-to-all-start = ((bf16[256,9,4,128]{3,2,1,0:T(4,128)(2,1)}), bf16[256,9,4,128]{3,2,1,0:T(4,128)(2,1)S(1)}, u32[]{:S(2)}, u32[]{:S(2)}) async-start(bf16[256,9,4,128]{3,2,1,0:T(4,128)(2,1)} %bitcast.1), calls=%async_computation | async-start | bytes 4718592 | tf_op jit(solution)/shard_map/all_to_all | solution.py:402
  70.0 0.1 copy.19
  70.1 0.1 maximum_bitcast_fusion.rate_ref
  70.2 0.1 select_maximum_fusion
  70.3 57.4 %all-to-all-done = bf16[256,9,4,128]{3,2,1,0:T(4,128)(2,1)S(1)} async-done(((bf16[256,9,4,128]{3,2,1,0:T(4,128)(2,1)}), bf16[256,9,4,128]{3,2,1,0:T(4,128)(2,1)S(1)}, u32[]{:S(2)}, u32[]{:S(2)}) %all-to-all-start) | async-done | bytes 2359328 | tf_op jit(solution)/shard_map/all_to_all | solution.py:402
  127.7 0.6 copy.18
  128.2 0.5 copy-done
  128.7 0.1 copy-done.1
  128.8 0.1 copy-done.2
  129.0 0.1 copy-done.3
  129.1 11.6 %shard_map.149 = f32[2,6,64,1536]{3,2,1,0:T(8,128)} custom-call(bf16[36,256,128]{2,1,0:T(8,128)(2,1)S(1)} %bitcast.8, f32[6]{0:T(128)S(1)} %multiply_multiply_fusion.wave_ref, bf16[512,512]{1,0:T(8,128)(2,1)S(1)} %copy-done, f32[3,256,128]{2,1,0:T(8,128)S(1)} %copy-done.3, f32[3,256,128]{2,1,0:T(8,128)S(1)} %copy-done.2, f32[3,256,128]{2,1,0:T(8,128)S(1)} %copy-done.1, ...), custom_call_target="tpu_custom_call" | custom-call | tf_op jit(solution)/shard_map/pallas_call | solution.py:429
  (26 shorter events, 0.1 us)
Async XLA Ops:
  0.7 0.8 copy-start.4
  1.5 0.8 copy-start.5
  2.3 0.7 copy-start.6
  4.8 6.9 %collective-permute-start = (bf16[208,384]{1,0:T(8,128)(2,1)S(1)}, bf16[208,384]{1,0:T(8,128)(2,1)S(1)}, u32[]{:S(2)}, u32[]{:S(2)}) collective-permute-start(bf16[208,384]{1,0:T(8,128)(2,1)S(1)} %get-tuple-element.20), channel_id=1, source_target_pairs={{0,8},{8,16},{16,24},{24,32},{32,40},{40,48},{48,56},{56,64},{64,7... | collective-permute-start | bytes 479240 | tf_op jit(solution)/shard_map/ppermute | solution.py:364
  4.9 42.7 %copy-start.7 = (bf16[512,1536]{1,0:T(8,128)(2,1)S(1)}, bf16[512,1536]{1,0:T(8,128)(2,1)}, u32[]{:S(2)}) copy-start(bf16[512,1536]{1,0:T(8,128)(2,1)} %constant.38.clone.refs_8_) | copy-start | bytes 4718596
  5.0 42.7 %copy-start.8 = (f32[3,256,128]{2,1,0:T(8,128)S(1)}, f32[3,256,128]{2,1,0:T(8,128)}, u32[]{:S(2)}) copy-start(f32[3,256,128]{2,1,0:T(8,128)} %constant.41.clone.refs_11_) | copy-start | bytes 1179652
  5.0 42.7 %copy-start.9 = (f32[3,256,128]{2,1,0:T(8,128)S(1)}, f32[3,256,128]{2,1,0:T(8,128)}, u32[]{:S(2)}) copy-start(f32[3,256,128]{2,1,0:T(8,128)} %constant.40.clone.refs_10_) | copy-start | bytes 1179652
  5.0 42.7 %copy-start.10 = (bf16[256,256]{1,0:T(8,128)(2,1)S(1)}, bf16[256,256]{1,0:T(8,128)(2,1)}, u32[]{:S(2)}) copy-start(bf16[256,256]{1,0:T(8,128)(2,1)} %constant.39.clone.refs_9_) | copy-start | bytes 393220
  12.2 14.2 %collective-permute-start.1 = (bf16[208,384]{1,0:T(8,128)(2,1)S(1)}, bf16[208,384]{1,0:T(8,128)(2,1)S(1)}, u32[]{:S(2)}, u32[]{:S(2)}) collective-permute-start(bf16[208,384]{1,0:T(8,128)(2,1)S(1)} %get-tuple-element.21), channel_id=1, source_target_pairs={{0,128},{8,137},{64,192},{72,201},{128,1},{136,8},{192,65},{200,72... | collective-permute-start | bytes 479240 | tf_op jit(solution)/shard_map/ppermute | solution.py:385
  15.5 14.8 %collective-permute-start.2 = (bf16[208,384]{1,0:T(8,128)(2,1)S(1)}, bf16[208,384]{1,0:T(8,128)(2,1)S(1)}, u32[]{:S(2)}, u32[]{:S(2)}) collective-permute-start(bf16[208,384]{1,0:T(8,128)(2,1)S(1)} %get-tuple-element.22), channel_id=1, source_target_pairs={{0,129},{8,136},{64,193},{72,200},{128,0},{136,9},{192,64},{200,73... | collective-permute-start | bytes 479240 | tf_op jit(solution)/shard_map/ppermute | solution.py:385
  18.6 20.2 %collective-permute-start.3 = (bf16[208,384]{1,0:T(8,128)(2,1)S(1)}, bf16[208,384]{1,0:T(8,128)(2,1)S(1)}, u32[]{:S(2)}, u32[]{:S(2)}) collective-permute-start(bf16[208,384]{1,0:T(8,128)(2,1)S(1)} %get-tuple-element.23), channel_id=1, source_target_pairs={{0,130},{8,139},{64,194},{72,203},{128,3},{136,10},{192,67},{200,7... | collective-permute-start | bytes 479240 | tf_op jit(solution)/shard_map/ppermute | solution.py:385
  22.0 19.7 %collective-permute-start.4 = (bf16[208,384]{1,0:T(8,128)(2,1)S(1)}, bf16[208,384]{1,0:T(8,128)(2,1)S(1)}, u32[]{:S(2)}, u32[]{:S(2)}) collective-permute-start(bf16[208,384]{1,0:T(8,128)(2,1)S(1)} %get-tuple-element.24), channel_id=1, source_target_pairs={{0,131},{8,138},{64,195},{72,202},{128,2},{136,11},{192,66},{200,7... | collective-permute-start | bytes 479240 | tf_op jit(solution)/shard_map/ppermute | solution.py:385
  23.7 20.1 %collective-permute-start.5 = (bf16[208,384]{1,0:T(8,128)(2,1)S(1)}, bf16[208,384]{1,0:T(8,128)(2,1)S(1)}, u32[]{:S(2)}, u32[]{:S(2)}) collective-permute-start(bf16[208,384]{1,0:T(8,128)(2,1)S(1)} %get-tuple-element.25), channel_id=1, source_target_pairs={{0,132},{8,141},{64,196},{72,205},{128,5},{136,12},{192,69},{200,7... | collective-permute-start | bytes 479240 | tf_op jit(solution)/shard_map/ppermute | solution.py:385
  26.4 17.5 %collective-permute-start.6 = (bf16[208,384]{1,0:T(8,128)(2,1)S(1)}, bf16[208,384]{1,0:T(8,128)(2,1)S(1)}, u32[]{:S(2)}, u32[]{:S(2)}) collective-permute-start(bf16[208,384]{1,0:T(8,128)(2,1)S(1)} %get-tuple-element.26), channel_id=1, source_target_pairs={{0,133},{8,140},{64,197},{72,204},{128,4},{136,13},{192,68},{200,7... | collective-permute-start | bytes 479240 | tf_op jit(solution)/shard_map/ppermute | solution.py:385
  30.3 16.1 %collective-permute-start.7 = (bf16[208,384]{1,0:T(8,128)(2,1)S(1)}, bf16[208,384]{1,0:T(8,128)(2,1)S(1)}, u32[]{:S(2)}, u32[]{:S(2)}) collective-permute-start(bf16[208,384]{1,0:T(8,128)(2,1)S(1)} %get-tuple-element.27), channel_id=1, source_target_pairs={{0,134},{8,143},{64,198},{72,207},{128,7},{136,14},{192,71},{200,7... | collective-permute-start | bytes 479240 | tf_op jit(solution)/shard_map/ppermute | solution.py:385
  38.7 8.9 %collective-permute-start.8 = (bf16[208,384]{1,0:T(8,128)(2,1)S(1)}, bf16[208,384]{1,0:T(8,128)(2,1)S(1)}, u32[]{:S(2)}, u32[]{:S(2)}) collective-permute-start(bf16[208,384]{1,0:T(8,128)(2,1)S(1)} %get-tuple-element.28), channel_id=1, source_target_pairs={{0,135},{8,142},{64,199},{72,206},{128,6},{136,15},{192,70},{200,7... | collective-permute-start | bytes 479240 | tf_op jit(solution)/shard_map/ppermute | solution.py:385
  54.3 15.7 %copy-start.11 = (f32[64,64]{1,0:T(8,128)S(1)}, f32[64,64]{1,0:T(8,128)}, u32[]{:S(2)}) copy-start(f32[64,64]{1,0:T(8,128)} %param.21) | copy-start | bytes 49156
  54.3 15.8 %copy-start.13 = (f32[64]{0:T(128)S(1)}, f32[64]{0:T(128)}, u32[]{:S(2)}) copy-start(f32[64]{0:T(128)} %param.19) | copy-start | bytes 772
  54.3 15.9 %copy-start.12 = (f32[64,64]{1,0:T(8,128)S(1)}, f32[64,64]{1,0:T(8,128)}, u32[]{:S(2)}) copy-start(f32[64,64]{1,0:T(8,128)} %param.20) | copy-start | bytes 49156
  54.3 73.4 %all-to-all-start = ((bf16[256,9,4,128]{3,2,1,0:T(4,128)(2,1)}), bf16[256,9,4,128]{3,2,1,0:T(4,128)(2,1)S(1)}, u32[]{:S(2)}, u32[]{:S(2)}) async-start(bf16[256,9,4,128]{3,2,1,0:T(4,128)(2,1)} %bitcast.1), calls=%async_computation | async-start | bytes 4718592 | tf_op jit(solution)/shard_map/all_to_all | solution.py:402
  127.7 1.0 copy-start
  127.7 1.2 copy-start.1
  127.7 1.3 copy-start.2
  127.7 1.4 copy-start.3

commit v4 on v3

--- a/solution.py
+++ b/solution.py
@@ -75,12 +75,35 @@
 
 
 def prepare_kernel(
-    count_ref, cell_ref, frac_ref, force_ref, right_ref, z_ref, x_ref, rim_ref, left_ref, sum_ref
+    count_ref,
+    cell_in,
+    frac_in,
+    force_in,
+    right_ref,
+    z_ref,
+    x_ref,
+    rim_ref,
+    cell_ref,
+    frac_ref,
+    force_ref,
+    left_ref,
+    sum_ref,
+    arrival,
 ):
+    copies = [
+        pltpu.make_async_copy(source, target, arrival.at[at])
+        for at, (source, target) in enumerate(
+            ((cell_in, cell_ref), (frac_in, frac_ref), (force_in, force_ref))
+        )
+    ]
+    for copy in copies:
+        copy.start()
     live_count = count_ref[0]
     capacity = force_ref.shape[1]
     scale = 8.0 / math.sqrt(capacity * 256)
     sum_ref[...] = jnp.zeros_like(sum_ref)
+    for copy in copies:
+        copy.wait()
 
     def body(block, carry):
         start = pl.multiple_of(block * NODE_BLOCK, NODE_BLOCK)
@@ -146,7 +169,7 @@
 
 def y_kernel(*refs):
     in_refs = refs[:8]
-    table_ref, flip_ref, cos_ref, sin_ref, out_ref, grid_ref, th_ref, tl_ref, mode_ref = refs[8:]
+    table_ref, flip_ref, cos_ref, sin_ref, out_ref, grid_ref, th_ref, mode_ref = refs[8:]
     for turn in range(8):
         start = pl.multiple_of(partner(turn, -1) * STRIP, STRIP)
         grid_ref[pl.ds(start, STRIP), :] = in_refs[turn][0:STRIP, :].astype(F32)
@@ -179,9 +202,7 @@
                     imag = jnp.zeros_like(real)
                 columns = slice(q * WIDTH + p * LANES, q * WIDTH + (p + 1) * LANES)
                 for at, value in ((0, real), (BASE, imag)):
-                    high, low = split_value(value)
-                    th_ref[pl.ds(at + start, 16), columns] = high
-                    tl_ref[pl.ds(at + start, 16), columns] = low
+                    th_ref[pl.ds(at + start, 16), columns] = value.astype(BF16)
         return carry
 
     lax.fori_loop(0, BASE // 16, body, 0, unroll=UNROLL_Y)
@@ -195,8 +216,7 @@
     for first in (1, 0, 2, 3):
         columns = slice(first * WIDTH, (first + 1) * WIDTH)
         high = th_ref[:, columns]
-        low = tl_ref[:, columns]
-        modes = matmul(table_ref[...], jnp.concatenate([high, high, low], axis=0))
+        modes = matmul(table_ref[...], high)
         for part in range(2):
             rows = modes[part * BASE : (part + 1) * BASE]
             put(first, part, rows, 0)
@@ -237,7 +257,7 @@
             ws_ref[LANES:, k * LANES : (k + 1) * LANES] = low
 
     lines = jnp.concatenate([in_ref[item] for item in range(6)], axis=1)
-    modes_ref[...] = matmul(table_ref[...], jnp.concatenate([lines, lines], axis=0))
+    modes_ref[...] = matmul(table_ref[...], lines)
     lane = lax.broadcasted_iota(jnp.int32, (16, LANES), 1)
     lower = lane < NZ
     sign = jnp.where(lower, 1.0, -1.0)
@@ -300,9 +320,9 @@
             out_ref[part, 0, :, (m + 3) * BASE : (m + 4) * BASE] = value[NZ:, columns]
 
 
-def vmem_call(kernel, inputs, out_shape, scratch_shapes, limit, scalars=1, cost=None):
+def vmem_call(kernel, inputs, out_shape, scratch_shapes, limit, scalars=1, cost=None, space=pltpu.VMEM):
     specs = [pl.BlockSpec(memory_space=pltpu.SMEM)] * scalars
-    specs += [pl.BlockSpec(memory_space=pltpu.VMEM)] * (len(inputs) - scalars)
+    specs += [pl.BlockSpec(memory_space=space)] * (len(inputs) - scalars)
     return pl.pallas_call(
         kernel,
         out_shape=out_shape,
@@ -337,13 +357,10 @@
     slabs = lax.axis_size("gx")
     cos_base, sin_base = base_tables()
     full = np.block([[cos_base, sin_base], [-sin_base, cos_base]])
-    high, low = split_table(full)
-    y_table = np.concatenate([high, low, high], axis=1)
+    y_table = split_table(full)[0]
     flip = np.eye(BASE)[::-1].astype(BF16)
     order = np.arange(BASE) ^ (BASE // 2)
-    x_table = np.concatenate(
-        split_table(np.concatenate([cos_base, sin_base], axis=0)[:, order]), axis=1
-    )
+    x_table = split_table(np.concatenate([cos_base, sin_base], axis=0)[:, order])[0]
 
     right, z_part, x_part, rim = vmem_call(
         prepare_kernel,
@@ -355,10 +372,15 @@
             jax.ShapeDtypeStruct((ROWS, RADIX * NZ), BF16),
         ),
         [
+            pltpu.VMEM((3, capacity), jnp.int32),
+            pltpu.VMEM((3, capacity), F32),
+            pltpu.VMEM((1, capacity), F32),
             pltpu.VMEM((RADIX * NZ, NODE_BLOCK), BF16),
             pltpu.VMEM((ROWS, RADIX * NZ), F32),
+            pltpu.SemaphoreType.DMA((3,)),
         ],
         PREPARE_BYTES,
+        space=pltpu.HBM,
         cost=pl.CostEstimate(flops=10**9, bytes_accessed=10**7, transcendentals=10**6),
     )
     rim = lax.ppermute(rim, "gx", [(i, (i + 1) % slabs) for i in range(slabs)])
@@ -390,7 +412,6 @@
         jax.ShapeDtypeStruct((BASE * ITEMS, LANES), BF16),
         [
             pltpu.VMEM((NY, WIDTH), F32),
-            pltpu.VMEM((2 * BASE, 4 * WIDTH), BF16),
             pltpu.VMEM((2 * BASE, 4 * WIDTH), BF16),
             pltpu.VMEM((BASE * ITEMS, LANES), F32),
         ],

time: 142 us -> 138 us (0.972)
  waiting for transfers between devices: 71.1 us -> 67.4 us
    pallas_call x4, Pallas kernels: 13 us -> 15.8 us  [vmem_call(): pl.pallas_call(kernel, out_shape=out_shape, in_specs=specs, out_specs=jax...]
    ppermute x1, waiting for transfers between devices: 2.62 us -> 0.01 us  [shards(): rim = lax.ppermute(rim, 'gx', [(i, (i + 1) % slabs) for i in range(slabs)])]
    pallas_call x1, Pallas kernels: 11.6 us -> 9.92 us  [shards(): pl.pallas_call(x_kernel, out_shape=jax.ShapeDtypeStruct((2, RADIX, NZ, NX...]
  transfers between devices with their start and end apart: 10 -> 10, of which waited for: 6 -> 4; matrix products, arithmetic and copies ran while one was open for 0% -> 0% of each run, Pallas kernels for 3% -> 6%
where the time goes in v4:
time: 138 us; the launch traced here: 137 us
  waiting for transfers between devices  67.4 us (49%)
  starting transfers between devices  39 us (28%)
  Pallas kernels  25.8 us (19%)
  local copies, waits for them, and re-layouts  3.79 us (3%)
    all_to_all x1, waiting for transfers between devices, shards(): lax.all_to_all(packed, BOTH, split_axis=0, concat_axis=0, tiled=True)  57.4 us
    ppermute x8, starting transfers between devices, shards(): lax.ppermute(part, BOTH, turn_route(dx, way))  24 us
    pallas_call x4, Pallas kernels, vmem_call(): pl.pallas_call(kernel, out_shape=out_shape, in_specs=specs, out_specs=jax...  15.8 us
    all_to_all x1, starting transfers between devices, shards(): lax.all_to_all(packed, BOTH, split_axis=0, concat_axis=0, tiled=True)  14.9 us
    ppermute x8, waiting for transfers between devices, shards(): lax.ppermute(part, BOTH, turn_route(dx, way))  10 us
    pallas_call x1, Pallas kernels, shards(): pl.pallas_call(x_kernel, out_shape=jax.ShapeDtypeStruct((2, RADIX, NZ, NX...  9.92 us
    unnamed x29, local copies, waits for them, and re-layouts  3.24 us
  transfers between devices with their start and end apart: 10, of which 4 were waited for; matrix products, arithmetic and copies ran while one was open for 0% of the time, Pallas kernels for 6%

profile of v4, /device:TPU:32, one launch (start us, length us, event | category | flops | bytes accessed | tf_op | source)
XLA Modules:
  0.0 137.0 jit_solution(17046106874761191214)
XLA Ops:
  0.7 0.8 copy-done.4
  1.5 0.8 copy-done.5
  2.3 0.7 copy-done.6
  3.1 3.7 %shard_map.145 = (bf16[208,4096]{1,0:T(8,128)(2,1)S(1)}, f32[64,4096]{1,0:T(8,128)S(1)}, f32[56,4096]{1,0:T(8,128)S(1)}, bf16[208,384]{1,0:T(8,128)(2,1)S(1)}) custom-call(s32[1]{0:T(128)S(6)} %copy.20.count_ref, s32[3,4096]{1,0:T(4,128)S(1)} %copy-done.4, f32[3,4096]{1,0:T(4,128)S(1)} %copy-done.5, f32[1,4096]{1,0:T(1,128)S(1)} %bitcast.9), custom_call_target="tpu_custom_call" | custom-call | flops 1000000000 | bytes 10000000 | tf_op jit(solution)/shard_map/pallas_call | solution.py:326
  6.8 0.1 collective-permute-start
  6.9 0.0 copy-start.8
  6.9 0.0 copy-start.9
  6.9 7.6 %shard_map.146.in_ref = bf16[8,208,384]{2,1,0:T(8,128)(2,1)S(1)} custom-call(s32[1]{0:T(128)S(6)} %copy.20.count_ref, bf16[208,4096]{1,0:T(8,128)(2,1)S(1)} %get-tuple-element.17.right_ref, f32[64,4096]{1,0:T(8,128)S(1)} %get-tuple-element.18.z_ref, f32[56,4096]{1,0:T(8,128)S(1)} %get-tuple-element.19.x_ref), custom_call_target="tpu_custom_call" | custom-call | flops 10000000000 | bytes 10000000 | tf_op jit(solution)/shard_map/pallas_call | solution.py:326
  14.5 0.4 shard_map.147
  15.0 3.3 %collective-permute-start.1 = (bf16[208,384]{1,0:T(8,128)(2,1)S(1)}, bf16[208,384]{1,0:T(8,128)(2,1)S(1)}, u32[]{:S(2)}, u32[]{:S(2)}) collective-permute-start(bf16[208,384]{1,0:T(8,128)(2,1)S(1)} %get-tuple-element.21), channel_id=1, source_target_pairs={{0,128},{8,137},{64,192},{72,201},{128,1},{136,8},{192,65},{200,72... | collective-permute-start | bytes 479240 | tf_op jit(solution)/shard_map/ppermute | solution.py:407
  18.3 0.9 collective-permute-start.2
  19.2 3.0 %collective-permute-start.3 = (bf16[208,384]{1,0:T(8,128)(2,1)S(1)}, bf16[208,384]{1,0:T(8,128)(2,1)S(1)}, u32[]{:S(2)}, u32[]{:S(2)}) collective-permute-start(bf16[208,384]{1,0:T(8,128)(2,1)S(1)} %get-tuple-element.23), channel_id=1, source_target_pairs={{0,130},{8,139},{64,194},{72,203},{128,3},{136,10},{192,67},{200,7... | collective-permute-start | bytes 479240 | tf_op jit(solution)/shard_map/ppermute | solution.py:407
  22.1 2.1 %collective-permute-start.4 = (bf16[208,384]{1,0:T(8,128)(2,1)S(1)}, bf16[208,384]{1,0:T(8,128)(2,1)S(1)}, u32[]{:S(2)}, u32[]{:S(2)}) collective-permute-start(bf16[208,384]{1,0:T(8,128)(2,1)S(1)} %get-tuple-element.24), channel_id=1, source_target_pairs={{0,131},{8,138},{64,195},{72,202},{128,2},{136,11},{192,66},{200,7... | collective-permute-start | bytes 479240 | tf_op jit(solution)/shard_map/ppermute | solution.py:407
  24.3 4.8 %collective-permute-start.5 = (bf16[208,384]{1,0:T(8,128)(2,1)S(1)}, bf16[208,384]{1,0:T(8,128)(2,1)S(1)}, u32[]{:S(2)}, u32[]{:S(2)}) collective-permute-start(bf16[208,384]{1,0:T(8,128)(2,1)S(1)} %get-tuple-element.25), channel_id=1, source_target_pairs={{0,132},{8,141},{64,196},{72,205},{128,5},{136,12},{192,69},{200,7... | collective-permute-start | bytes 479240 | tf_op jit(solution)/shard_map/ppermute | solution.py:407
  29.1 3.4 %collective-permute-start.6 = (bf16[208,384]{1,0:T(8,128)(2,1)S(1)}, bf16[208,384]{1,0:T(8,128)(2,1)S(1)}, u32[]{:S(2)}, u32[]{:S(2)}) collective-permute-start(bf16[208,384]{1,0:T(8,128)(2,1)S(1)} %get-tuple-element.26), channel_id=1, source_target_pairs={{0,133},{8,140},{64,197},{72,204},{128,4},{136,13},{192,68},{200,7... | collective-permute-start | bytes 479240 | tf_op jit(solution)/shard_map/ppermute | solution.py:407
  32.5 2.3 %collective-permute-start.7 = (bf16[208,384]{1,0:T(8,128)(2,1)S(1)}, bf16[208,384]{1,0:T(8,128)(2,1)S(1)}, u32[]{:S(2)}, u32[]{:S(2)}) collective-permute-start(bf16[208,384]{1,0:T(8,128)(2,1)S(1)} %get-tuple-element.27), channel_id=1, source_target_pairs={{0,134},{8,143},{64,198},{72,207},{128,7},{136,14},{192,71},{200,7... | collective-permute-start | bytes 479240 | tf_op jit(solution)/shard_map/ppermute | solution.py:407
  34.8 4.1 %collective-permute-start.8 = (bf16[208,384]{1,0:T(8,128)(2,1)S(1)}, bf16[208,384]{1,0:T(8,128)(2,1)S(1)}, u32[]{:S(2)}, u32[]{:S(2)}) collective-permute-start(bf16[208,384]{1,0:T(8,128)(2,1)S(1)} %get-tuple-element.28), channel_id=1, source_target_pairs={{0,135},{8,142},{64,199},{72,206},{128,6},{136,15},{192,70},{200,7... | collective-permute-start | bytes 479240 | tf_op jit(solution)/shard_map/ppermute | solution.py:407
  39.0 0.7 collective-permute-done.5.refs_4_
  39.7 4.1 %collective-permute-done.6.refs_5_ = bf16[208,384]{1,0:T(8,128)(2,1)S(1)} collective-permute-done((bf16[208,384]{1,0:T(8,128)(2,1)S(1)}, bf16[208,384]{1,0:T(8,128)(2,1)S(1)}, u32[]{:S(2)}, u32[]{:S(2)}) %collective-permute-start.6) | collective-permute-done | bytes 159776 | tf_op jit(solution)/shard_map/ppermute | solution.py:407
  43.7 5.3 %collective-permute-done.7.refs_6_ = bf16[208,384]{1,0:T(8,128)(2,1)S(1)} collective-permute-done((bf16[208,384]{1,0:T(8,128)(2,1)S(1)}, bf16[208,384]{1,0:T(8,128)(2,1)S(1)}, u32[]{:S(2)}, u32[]{:S(2)}) %collective-permute-start.7) | collective-permute-done | bytes 159776 | tf_op jit(solution)/shard_map/ppermute | solution.py:407
  49.0 4.1 %shard_map.148 = bf16[9216,128]{1,0:T(8,128)(2,1)} custom-call(bf16[208,384]{1,0:T(8,128)(2,1)S(1)} %collective-permute-done.1.refs_0_, bf16[208,384]{1,0:T(8,128)(2,1)S(1)} %collective-permute-done.2.refs_1_, bf16[208,384]{1,0:T(8,128)(2,1)S(1)} %collective-permute-done.3.refs_2_, bf16[208,384]{1,0:T(8,128)(2,1)S(1)} %collective-permute-done.4.refs_3_, ...), custom_call_target="tpu_custom_call" | custom-call | flops 5000000000 | bytes 10000000 | tf_op jit(solution)/shard_map/pallas_call | solution.py:326
  53.1 14.9 %all-to-all-start = ((bf16[256,9,4,128]{3,2,1,0:T(4,128)(2,1)}), bf16[256,9,4,128]{3,2,1,0:T(4,128)(2,1)S(1)}, u32[]{:S(2)}, u32[]{:S(2)}) async-start(bf16[256,9,4,128]{3,2,1,0:T(4,128)(2,1)} %bitcast.1), calls=%async_computation | async-start | bytes 4718592 | tf_op jit(solution)/shard_map/all_to_all | solution.py:423
  68.1 0.1 copy.19
  68.2 0.1 maximum_bitcast_fusion.rate_ref
  68.3 0.1 select_maximum_fusion
  68.4 57.4 %all-to-all-done = bf16[256,9,4,128]{3,2,1,0:T(4,128)(2,1)S(1)} async-done(((bf16[256,9,4,128]{3,2,1,0:T(4,128)(2,1)}), bf16[256,9,4,128]{3,2,1,0:T(4,128)(2,1)S(1)}, u32[]{:S(2)}, u32[]{:S(2)}) %all-to-all-start) | async-done | bytes 2359328 | tf_op jit(solution)/shard_map/all_to_all | solution.py:423
  125.8 0.6 copy.18
  126.3 0.4 copy-done
  126.8 0.1 copy-done.1
  126.9 0.1 copy-done.2
  127.0 0.1 copy-done.3
  127.1 9.9 %shard_map.149 = f32[2,6,64,1536]{3,2,1,0:T(8,128)} custom-call(bf16[36,256,128]{2,1,0:T(8,128)(2,1)S(1)} %bitcast.8, f32[6]{0:T(128)S(1)} %multiply_multiply_fusion.wave_ref, bf16[512,256]{1,0:T(8,128)(2,1)S(1)} %copy-done.3, f32[3,256,128]{2,1,0:T(8,128)S(1)} %copy-done.2, f32[3,256,128]{2,1,0:T(8,128)S(1)} %copy-done.1, f32[3,256,128]{2,1,0:T(8,128)S(1)} %copy-done, ...), custom_call_target="tpu_custom_call" | custom-call | tf_op jit(solution)/shard_map/pallas_call | solution.py:450
  (26 shorter events, 0.1 us)
Async XLA Ops:
  0.7 0.8 copy-start.4
  1.5 0.8 copy-start.5
  2.3 0.7 copy-start.6
  6.8 7.7 %collective-permute-start = (bf16[208,384]{1,0:T(8,128)(2,1)S(1)}, bf16[208,384]{1,0:T(8,128)(2,1)S(1)}, u32[]{:S(2)}, u32[]{:S(2)}) collective-permute-start(bf16[208,384]{1,0:T(8,128)(2,1)S(1)} %get-tuple-element.20), channel_id=1, source_target_pairs={{0,8},{8,16},{16,24},{24,32},{32,40},{40,48},{48,56},{56,64},{64,7... | collective-permute-start | bytes 479240 | tf_op jit(solution)/shard_map/ppermute | solution.py:386
  6.9 42.1 %copy-start.7 = (bf16[512,512]{1,0:T(8,128)(2,1)S(1)}, bf16[512,512]{1,0:T(8,128)(2,1)}, u32[]{:S(2)}) copy-start(bf16[512,512]{1,0:T(8,128)(2,1)} %constant.38.clone.refs_8_) | copy-start | bytes 1572868
  6.9 42.1 %copy-start.8 = (f32[3,256,128]{2,1,0:T(8,128)S(1)}, f32[3,256,128]{2,1,0:T(8,128)}, u32[]{:S(2)}) copy-start(f32[3,256,128]{2,1,0:T(8,128)} %constant.41.clone.refs_11_) | copy-start | bytes 1179652
  6.9 42.1 %copy-start.9 = (f32[3,256,128]{2,1,0:T(8,128)S(1)}, f32[3,256,128]{2,1,0:T(8,128)}, u32[]{:S(2)}) copy-start(f32[3,256,128]{2,1,0:T(8,128)} %constant.40.clone.refs_10_) | copy-start | bytes 1179652
  6.9 42.1 %copy-start.10 = (bf16[256,256]{1,0:T(8,128)(2,1)S(1)}, bf16[256,256]{1,0:T(8,128)(2,1)}, u32[]{:S(2)}) copy-start(bf16[256,256]{1,0:T(8,128)(2,1)} %constant.39.clone.refs_9_) | copy-start | bytes 393220
  15.0 14.1 %collective-permute-start.1 = (bf16[208,384]{1,0:T(8,128)(2,1)S(1)}, bf16[208,384]{1,0:T(8,128)(2,1)S(1)}, u32[]{:S(2)}, u32[]{:S(2)}) collective-permute-start(bf16[208,384]{1,0:T(8,128)(2,1)S(1)} %get-tuple-element.21), channel_id=1, source_target_pairs={{0,128},{8,137},{64,192},{72,201},{128,1},{136,8},{192,65},{200,72... | collective-permute-start | bytes 479240 | tf_op jit(solution)/shard_map/ppermute | solution.py:407
  18.3 14.2 %collective-permute-start.2 = (bf16[208,384]{1,0:T(8,128)(2,1)S(1)}, bf16[208,384]{1,0:T(8,128)(2,1)S(1)}, u32[]{:S(2)}, u32[]{:S(2)}) collective-permute-start(bf16[208,384]{1,0:T(8,128)(2,1)S(1)} %get-tuple-element.22), channel_id=1, source_target_pairs={{0,129},{8,136},{64,193},{72,200},{128,0},{136,9},{192,64},{200,73... | collective-permute-start | bytes 479240 | tf_op jit(solution)/shard_map/ppermute | solution.py:407
  19.2 15.7 %collective-permute-start.3 = (bf16[208,384]{1,0:T(8,128)(2,1)S(1)}, bf16[208,384]{1,0:T(8,128)(2,1)S(1)}, u32[]{:S(2)}, u32[]{:S(2)}) collective-permute-start(bf16[208,384]{1,0:T(8,128)(2,1)S(1)} %get-tuple-element.23), channel_id=1, source_target_pairs={{0,130},{8,139},{64,194},{72,203},{128,3},{136,10},{192,67},{200,7... | collective-permute-start | bytes 479240 | tf_op jit(solution)/shard_map/ppermute | solution.py:407
  22.1 16.8 %collective-permute-start.4 = (bf16[208,384]{1,0:T(8,128)(2,1)S(1)}, bf16[208,384]{1,0:T(8,128)(2,1)S(1)}, u32[]{:S(2)}, u32[]{:S(2)}) collective-permute-start(bf16[208,384]{1,0:T(8,128)(2,1)S(1)} %get-tuple-element.24), channel_id=1, source_target_pairs={{0,131},{8,138},{64,195},{72,202},{128,2},{136,11},{192,66},{200,7... | collective-permute-start | bytes 479240 | tf_op jit(solution)/shard_map/ppermute | solution.py:407
  24.3 15.4 %collective-permute-start.5 = (bf16[208,384]{1,0:T(8,128)(2,1)S(1)}, bf16[208,384]{1,0:T(8,128)(2,1)S(1)}, u32[]{:S(2)}, u32[]{:S(2)}) collective-permute-start(bf16[208,384]{1,0:T(8,128)(2,1)S(1)} %get-tuple-element.25), channel_id=1, source_target_pairs={{0,132},{8,141},{64,196},{72,205},{128,5},{136,12},{192,69},{200,7... | collective-permute-start | bytes 479240 | tf_op jit(solution)/shard_map/ppermute | solution.py:407
  29.1 14.6 %collective-permute-start.6 = (bf16[208,384]{1,0:T(8,128)(2,1)S(1)}, bf16[208,384]{1,0:T(8,128)(2,1)S(1)}, u32[]{:S(2)}, u32[]{:S(2)}) collective-permute-start(bf16[208,384]{1,0:T(8,128)(2,1)S(1)} %get-tuple-element.26), channel_id=1, source_target_pairs={{0,133},{8,140},{64,197},{72,204},{128,4},{136,13},{192,68},{200,7... | collective-permute-start | bytes 479240 | tf_op jit(solution)/shard_map/ppermute | solution.py:407
  32.5 16.5 %collective-permute-start.7 = (bf16[208,384]{1,0:T(8,128)(2,1)S(1)}, bf16[208,384]{1,0:T(8,128)(2,1)S(1)}, u32[]{:S(2)}, u32[]{:S(2)}) collective-permute-start(bf16[208,384]{1,0:T(8,128)(2,1)S(1)} %get-tuple-element.27), channel_id=1, source_target_pairs={{0,134},{8,143},{64,198},{72,207},{128,7},{136,14},{192,71},{200,7... | collective-permute-start | bytes 479240 | tf_op jit(solution)/shard_map/ppermute | solution.py:407
  34.8 14.2 %collective-permute-start.8 = (bf16[208,384]{1,0:T(8,128)(2,1)S(1)}, bf16[208,384]{1,0:T(8,128)(2,1)S(1)}, u32[]{:S(2)}, u32[]{:S(2)}) collective-permute-start(bf16[208,384]{1,0:T(8,128)(2,1)S(1)} %get-tuple-element.28), channel_id=1, source_target_pairs={{0,135},{8,142},{64,199},{72,206},{128,6},{136,15},{192,70},{200,7... | collective-permute-start | bytes 479240 | tf_op jit(solution)/shard_map/ppermute | solution.py:407
  53.1 15.0 %copy-start.11 = (f32[64,64]{1,0:T(8,128)S(1)}, f32[64,64]{1,0:T(8,128)}, u32[]{:S(2)}) copy-start(f32[64,64]{1,0:T(8,128)} %param.21) | copy-start | bytes 49156
  53.1 15.1 %copy-start.13 = (f32[64]{0:T(128)S(1)}, f32[64]{0:T(128)}, u32[]{:S(2)}) copy-start(f32[64]{0:T(128)} %param.19) | copy-start | bytes 772
  53.1 15.2 %copy-start.12 = (f32[64,64]{1,0:T(8,128)S(1)}, f32[64,64]{1,0:T(8,128)}, u32[]{:S(2)}) copy-start(f32[64,64]{1,0:T(8,128)} %param.20) | copy-start | bytes 49156
  53.1 72.6 %all-to-all-start = ((bf16[256,9,4,128]{3,2,1,0:T(4,128)(2,1)}), bf16[256,9,4,128]{3,2,1,0:T(4,128)(2,1)S(1)}, u32[]{:S(2)}, u32[]{:S(2)}) async-start(bf16[256,9,4,128]{3,2,1,0:T(4,128)(2,1)} %bitcast.1), calls=%async_computation | async-start | bytes 4718592 | tf_op jit(solution)/shard_map/all_to_all | solution.py:423
  125.8 1.0 copy-start
  125.8 1.1 copy-start.1
  125.8 1.2 copy-start.2
  125.8 1.3 copy-start.3

commit v5 on v4

--- a/solution.py
+++ b/solution.py
@@ -26,7 +26,7 @@
 ITEMS = 36
 WIDTH = 384
 BOTH = ("gx", "gy")
-TURNS = tuple((dx, way) for dx in range(4) for way in range(2))
+TURNS = tuple((dx, way) for dx in (2, 1, 3, 0) for way in range(2))
 F32 = jnp.float32
 BF16 = jnp.bfloat16
 HALF_ROOT3 = math.sqrt(3.0) / 2.0
@@ -256,8 +256,6 @@
             ws_ref[:LANES, k * LANES : (k + 1) * LANES] = high
             ws_ref[LANES:, k * LANES : (k + 1) * LANES] = low
 
-    lines = jnp.concatenate([in_ref[item] for item in range(6)], axis=1)
-    modes_ref[...] = matmul(table_ref[...], lines)
     lane = lax.broadcasted_iota(jnp.int32, (16, LANES), 1)
     lower = lane < NZ
     sign = jnp.where(lower, 1.0, -1.0)
@@ -265,59 +263,66 @@
     turn_2r = jnp.where(lower, 1.0, -0.5)
     turn_i = jnp.where(lower, 0.0, -HALF_ROOT3)
 
-    def body(step, carry):
-        start = pl.multiple_of(step * 16, 16)
-        real, imag = [], []
-        for xp in range(3):
-            at_real = slice(xp * LANES, (xp + 1) * LANES)
-            at_imag = slice((3 + xp) * LANES, (4 + xp) * LANES)
-            mode_real = (
-                modes_ref[pl.ds(start, 16), at_real] + modes_ref[pl.ds(BASE + start, 16), at_imag]
+    def one_wave(k):
+        lines = jnp.concatenate([in_ref[6 * k + item] for item in range(6)], axis=1)
+        modes_ref[k] = matmul(table_ref[...], lines)
+
+        def body(step, carry):
+            start = pl.multiple_of(step * 16, 16)
+            real, imag = [], []
+            for xp in range(3):
+                at_real = slice(xp * LANES, (xp + 1) * LANES)
+                at_imag = slice((3 + xp) * LANES, (4 + xp) * LANES)
+                mode_real = (
+                    modes_ref[k, pl.ds(start, 16), at_real] + modes_ref[k, pl.ds(BASE + start, 16), at_imag]
+                )
+                mode_imag = (
+                    modes_ref[k, pl.ds(start, 16), at_imag] - modes_ref[k, pl.ds(BASE + start, 16), at_real]
+                )
+                cos = cos_ref[xp, pl.ds(start, 16), :]
+                sin = sin_ref[xp, pl.ds(start, 16), :]
+                real.append(mode_real * cos + mode_imag * sin)
+                imag.append(mode_imag * cos - mode_real * sin)
+            sum_r, sum_i = real[1] + real[2], imag[1] + imag[2]
+            dif_r, dif_i = HALF_ROOT3 * (real[1] - real[2]), HALF_ROOT3 * (imag[1] - imag[2])
+            mid_r, mid_i = real[0] - 0.5 * sum_r, imag[0] - 0.5 * sum_i
+            u1r, u1i = mid_r + dif_i, mid_i - dif_r
+            u2r, u2i = mid_r - dif_i, mid_i + dif_r
+            thirds = (
+                (real[0] + sum_r, imag[0] + sum_i),
+                (u1r * turn_1r - u1i * turn_i, u1i * turn_1r + u1r * turn_i),
+                (u2r * turn_2r - u2i * turn_i, u2i * turn_2r + u2r * turn_i),
             )
-            mode_imag = (
-                modes_ref[pl.ds(start, 16), at_imag] - modes_ref[pl.ds(BASE + start, 16), at_real]
-            )
-            cos = cos_ref[xp, pl.ds(start, 16), :]
-            sin = sin_ref[xp, pl.ds(start, 16), :]
-            real.append(mode_real * cos + mode_imag * sin)
-            imag.append(mode_imag * cos - mode_real * sin)
-        sum_r, sum_i = real[1] + real[2], imag[1] + imag[2]
-        dif_r, dif_i = HALF_ROOT3 * (real[1] - real[2]), HALF_ROOT3 * (imag[1] - imag[2])
-        mid_r, mid_i = real[0] - 0.5 * sum_r, imag[0] - 0.5 * sum_i
-        u1r, u1i = mid_r + dif_i, mid_i - dif_r
-        u2r, u2i = mid_r - dif_i, mid_i + dif_r
-        thirds = (
-            (real[0] + sum_r, imag[0] + sum_i),
-            (u1r * turn_1r - u1i * turn_i, u1i * turn_1r + u1r * turn_i),
-            (u2r * turn_2r - u2i * turn_i, u2i * turn_2r + u2r * turn_i),
-        )
+            for m in range(3):
+                for part in range(2):
+                    value = thirds[m][part]
+                    value = pltpu.roll(value, NZ, 1) + sign * value
+                    high, low = split_value(value)
+                    row = pl.ds((m * 2 + part) * BASE + start, 16)
+                    x_ref[k, row, :LANES] = high
+                    x_ref[k, row, LANES:] = low
+            return carry
+
+        lax.fori_loop(0, BASE // 16, body, 0, unroll=UNROLL_X)
+        shift = rate_ref[...] + wave_ref[2 * q + k]
+        both = matmul(x_ref[k], wa_ref[...])
+        for m in range(3):
+            inverse = 1.0 / (across_ref[m] + shift)
+            for part in range(2):
+                rows = slice((m * 2 + part) * BASE, (m * 2 + part + 1) * BASE)
+                high, low = split_value((both[rows, :LANES] + both[rows, LANES:]) * inverse)
+                c_ref[k, rows, :LANES] = high
+                c_ref[k, rows, LANES:] = low
+        both = dot_rows(ws_ref[...], c_ref[k])
+        value = both[:LANES] + both[LANES:]
         for m in range(3):
             for part in range(2):
-                value = thirds[m][part]
-                value = pltpu.roll(value, NZ, 1) + sign * value
-                high, low = split_value(value)
-                row = pl.ds((m * 2 + part) * BASE + start, 16)
-                x_ref[row, :LANES] = high
-                x_ref[row, LANES:] = low
-        return carry
-
-    lax.fori_loop(0, BASE // 16, body, 0, unroll=UNROLL_X)
-    shift = rate_ref[...] + wave_ref[q]
-    both = matmul(x_ref[...], wa_ref[...])
-    for m in range(3):
-        inverse = 1.0 / (across_ref[m] + shift)
-        for part in range(2):
-            rows = slice((m * 2 + part) * BASE, (m * 2 + part + 1) * BASE)
-            high, low = split_value((both[rows, :LANES] + both[rows, LANES:]) * inverse)
-            c_ref[rows, :LANES] = high
-            c_ref[rows, LANES:] = low
-    both = dot_rows(ws_ref[...], c_ref[...])
-    value = both[:LANES] + both[LANES:]
-    for m in range(3):
-        for part in range(2):
-            columns = slice((m * 2 + part) * BASE, (m * 2 + part + 1) * BASE)
-            out_ref[part, 0, :, m * BASE : (m + 1) * BASE] = value[:NZ, columns]
-            out_ref[part, 0, :, (m + 3) * BASE : (m + 4) * BASE] = value[NZ:, columns]
+                columns = slice((m * 2 + part) * BASE, (m * 2 + part + 1) * BASE)
+                out_ref[part, k, :, m * BASE : (m + 1) * BASE] = value[:NZ, columns]
+                out_ref[part, k, :, (m + 3) * BASE : (m + 4) * BASE] = value[NZ:, columns]
+
+    for k in range(2):
+        one_wave(k)
 
 
 def vmem_call(kernel, inputs, out_shape, scratch_shapes, limit, scalars=1, cost=None, space=pltpu.VMEM):
@@ -450,15 +455,15 @@
     out = pl.pallas_call(
         x_kernel,
         out_shape=jax.ShapeDtypeStruct((2, RADIX, NZ, NX), F32),
-        grid=(RADIX,),
-        in_specs=[pl.BlockSpec((6, BASE, LANES), lambda q: (q, 0, 0))]
+        grid=(RADIX // 2,),
+        in_specs=[pl.BlockSpec((12, BASE, LANES), lambda q: (q, 0, 0))]
         + [pl.BlockSpec(memory_space=pltpu.SMEM)]
         + [whole(array) for array in constants],
-        out_specs=pl.BlockSpec((2, 1, NZ, NX), lambda q: (0, q, 0, 0)),
+        out_specs=pl.BlockSpec((2, 2, NZ, NX), lambda q: (0, q, 0, 0)),
         scratch_shapes=[
-            pltpu.VMEM((2 * BASE, RADIX * LANES), F32),
-            pltpu.VMEM((RADIX * BASE, 2 * LANES), BF16),
-            pltpu.VMEM((RADIX * BASE, 2 * LANES), BF16),
+            pltpu.VMEM((2, 2 * BASE, RADIX * LANES), F32),
+            pltpu.VMEM((2, RADIX * BASE, 2 * LANES), BF16),
+            pltpu.VMEM((2, RADIX * BASE, 2 * LANES), BF16),
             pltpu.VMEM((2 * LANES, 2 * LANES), BF16),
             pltpu.VMEM((2 * LANES, 2 * LANES), BF16),
         ],

time: 138 us -> 134 us (0.971)
  Pallas kernels: 25.8 us -> 20.2 us
  waiting for transfers between devices: 67.4 us -> 72 us
  starting transfers between devices: 39 us -> 35.5 us
    pallas_call x4, Pallas kernels: 15.8 us -> 10.6 us  [vmem_call(): pl.pallas_call(kernel, out_shape=out_shape, in_specs=specs, out_specs=jax...]
    all_to_all x1, starting transfers between devices: 14.9 us -> 10.5 us  [shards(): lax.all_to_all(packed, BOTH, split_axis=0, concat_axis=0, tiled=True)]
    ppermute x1, waiting for transfers between devices: 0.01 us -> 2.62 us  [shards(): rim = lax.ppermute(rim, 'gx', [(i, (i + 1) % slabs) for i in range(slabs)])]
    ppermute x8, waiting for transfers between devices: 10 us -> 12 us  [shards(): lax.ppermute(part, BOTH, turn_route(dx, way))]
  transfers between devices with their start and end apart: 10 -> 10, of which waited for: 4 -> 7; matrix products, arithmetic and copies ran while one was open for 0% -> 0% of each run, Pallas kernels for 6% -> 3%
where the time goes in v5:
time: 134 us; the launch traced here: 132 us
  waiting for transfers between devices  72 us (54%)
  starting transfers between devices  35.5 us (26%)
  Pallas kernels  20.2 us (15%)
  local copies, waits for them, and re-layouts  3.79 us (3%)
    all_to_all x1, waiting for transfers between devices, shards(): lax.all_to_all(packed, BOTH, split_axis=0, concat_axis=0, tiled=True)  57.4 us
    ppermute x8, starting transfers between devices, shards(): lax.ppermute(part, BOTH, turn_route(dx, way))  24.9 us
    ppermute x8, waiting for transfers between devices, shards(): lax.ppermute(part, BOTH, turn_route(dx, way))  12 us
    pallas_call x4, Pallas kernels, vmem_call(): pl.pallas_call(kernel, out_shape=out_shape, in_specs=specs, out_specs=jax...  10.6 us
    all_to_all x1, starting transfers between devices, shards(): lax.all_to_all(packed, BOTH, split_axis=0, concat_axis=0, tiled=True)  10.5 us
    pallas_call x1, Pallas kernels, shards(): pl.pallas_call(x_kernel, out_shape=jax.ShapeDtypeStruct((2, RADIX, NZ, NX...  9.55 us
    unnamed x29, local copies, waits for them, and re-layouts  3.24 us
  transfers between devices with their start and end apart: 10, of which 7 were waited for; matrix products, arithmetic and copies ran while one was open for 0% of the time, Pallas kernels for 3%

profile of v5, /device:TPU:32, one launch (start us, length us, event | category | flops | bytes accessed | tf_op | source)
XLA Modules:
  0.0 132.5 jit_solution(10429024944504464371)
XLA Ops:
  0.7 0.8 copy-done.4
  1.5 0.8 copy-done.5
  2.3 0.7 copy-done.6
  3.1 2.0 %shard_map.145 = (bf16[208,4096]{1,0:T(8,128)(2,1)S(1)}, f32[64,4096]{1,0:T(8,128)S(1)}, f32[56,4096]{1,0:T(8,128)S(1)}, bf16[208,384]{1,0:T(8,128)(2,1)S(1)}) custom-call(s32[1]{0:T(128)S(6)} %copy.20.count_ref, s32[3,4096]{1,0:T(4,128)S(1)} %copy-done.4, f32[3,4096]{1,0:T(4,128)S(1)} %copy-done.5, f32[1,4096]{1,0:T(1,128)S(1)} %bitcast.9), custom_call_target="tpu_custom_call" | custom-call | flops 1000000000 | bytes 10000000 | tf_op jit(solution)/shard_map/pallas_call | solution.py:331
  5.0 0.1 collective-permute-start
  5.2 4.1 %shard_map.146.in_ref = bf16[8,208,384]{2,1,0:T(8,128)(2,1)S(1)} custom-call(s32[1]{0:T(128)S(6)} %copy.20.count_ref, bf16[208,4096]{1,0:T(8,128)(2,1)S(1)} %get-tuple-element.17.right_ref, f32[64,4096]{1,0:T(8,128)S(1)} %get-tuple-element.18.z_ref, f32[56,4096]{1,0:T(8,128)S(1)} %get-tuple-element.19.x_ref), custom_call_target="tpu_custom_call" | custom-call | flops 10000000000 | bytes 10000000 | tf_op jit(solution)/shard_map/pallas_call | solution.py:331
  9.3 2.6 %collective-permute-done.rim_ref = bf16[208,384]{1,0:T(8,128)(2,1)S(1)} collective-permute-done((bf16[208,384]{1,0:T(8,128)(2,1)S(1)}, bf16[208,384]{1,0:T(8,128)(2,1)S(1)}, u32[]{:S(2)}, u32[]{:S(2)}) %collective-permute-start) | collective-permute-done | bytes 159776 | tf_op jit(solution)/shard_map/ppermute | solution.py:391
  11.9 0.4 shard_map.147
  12.4 5.8 %collective-permute-start.1 = (bf16[208,384]{1,0:T(8,128)(2,1)S(1)}, bf16[208,384]{1,0:T(8,128)(2,1)S(1)}, u32[]{:S(2)}, u32[]{:S(2)}) collective-permute-start(bf16[208,384]{1,0:T(8,128)(2,1)S(1)} %get-tuple-element.21), channel_id=1, source_target_pairs={{0,132},{8,141},{64,196},{72,205},{128,5},{136,12},{192,69},{200,7... | collective-permute-start | bytes 479240 | tf_op jit(solution)/shard_map/ppermute | solution.py:412
  18.2 2.2 %collective-permute-start.2 = (bf16[208,384]{1,0:T(8,128)(2,1)S(1)}, bf16[208,384]{1,0:T(8,128)(2,1)S(1)}, u32[]{:S(2)}, u32[]{:S(2)}) collective-permute-start(bf16[208,384]{1,0:T(8,128)(2,1)S(1)} %get-tuple-element.22), channel_id=1, source_target_pairs={{0,133},{8,140},{64,197},{72,204},{128,4},{136,13},{192,68},{200,7... | collective-permute-start | bytes 479240 | tf_op jit(solution)/shard_map/ppermute | solution.py:412
  20.4 1.6 %collective-permute-start.3 = (bf16[208,384]{1,0:T(8,128)(2,1)S(1)}, bf16[208,384]{1,0:T(8,128)(2,1)S(1)}, u32[]{:S(2)}, u32[]{:S(2)}) collective-permute-start(bf16[208,384]{1,0:T(8,128)(2,1)S(1)} %get-tuple-element.23), channel_id=1, source_target_pairs={{0,130},{8,139},{64,194},{72,203},{128,3},{136,10},{192,67},{200,7... | collective-permute-start | bytes 479240 | tf_op jit(solution)/shard_map/ppermute | solution.py:412
  22.0 3.0 %collective-permute-start.4 = (bf16[208,384]{1,0:T(8,128)(2,1)S(1)}, bf16[208,384]{1,0:T(8,128)(2,1)S(1)}, u32[]{:S(2)}, u32[]{:S(2)}) collective-permute-start(bf16[208,384]{1,0:T(8,128)(2,1)S(1)} %get-tuple-element.24), channel_id=1, source_target_pairs={{0,131},{8,138},{64,195},{72,202},{128,2},{136,11},{192,66},{200,7... | collective-permute-start | bytes 479240 | tf_op jit(solution)/shard_map/ppermute | solution.py:412
  25.0 3.0 %collective-permute-start.5 = (bf16[208,384]{1,0:T(8,128)(2,1)S(1)}, bf16[208,384]{1,0:T(8,128)(2,1)S(1)}, u32[]{:S(2)}, u32[]{:S(2)}) collective-permute-start(bf16[208,384]{1,0:T(8,128)(2,1)S(1)} %get-tuple-element.25), channel_id=1, source_target_pairs={{0,134},{8,143},{64,198},{72,207},{128,7},{136,14},{192,71},{200,7... | collective-permute-start | bytes 479240 | tf_op jit(solution)/shard_map/ppermute | solution.py:412
  28.0 6.8 %collective-permute-start.6 = (bf16[208,384]{1,0:T(8,128)(2,1)S(1)}, bf16[208,384]{1,0:T(8,128)(2,1)S(1)}, u32[]{:S(2)}, u32[]{:S(2)}) collective-permute-start(bf16[208,384]{1,0:T(8,128)(2,1)S(1)} %get-tuple-element.26), channel_id=1, source_target_pairs={{0,135},{8,142},{64,199},{72,206},{128,6},{136,15},{192,70},{200,7... | collective-permute-start | bytes 479240 | tf_op jit(solution)/shard_map/ppermute | solution.py:412
  34.8 1.6 %collective-permute-done.3.refs_2_ = bf16[208,384]{1,0:T(8,128)(2,1)S(1)} collective-permute-done((bf16[208,384]{1,0:T(8,128)(2,1)S(1)}, bf16[208,384]{1,0:T(8,128)(2,1)S(1)}, u32[]{:S(2)}, u32[]{:S(2)}) %collective-permute-start.3) | collective-permute-done | bytes 159776 | tf_op jit(solution)/shard_map/ppermute | solution.py:412
  36.4 2.5 %collective-permute-start.8 = (bf16[208,384]{1,0:T(8,128)(2,1)S(1)}, bf16[208,384]{1,0:T(8,128)(2,1)S(1)}, u32[]{:S(2)}, u32[]{:S(2)}) collective-permute-start(bf16[208,384]{1,0:T(8,128)(2,1)S(1)} %get-tuple-element.28), channel_id=1, source_target_pairs={{0,129},{8,136},{64,193},{72,200},{128,0},{136,9},{192,64},{200,73... | collective-permute-start | bytes 479240 | tf_op jit(solution)/shard_map/ppermute | solution.py:412
  38.9 0.4 collective-permute-done.5.refs_4_
  39.3 4.2 %collective-permute-done.6.refs_5_ = bf16[208,384]{1,0:T(8,128)(2,1)S(1)} collective-permute-done((bf16[208,384]{1,0:T(8,128)(2,1)S(1)}, bf16[208,384]{1,0:T(8,128)(2,1)S(1)}, u32[]{:S(2)}, u32[]{:S(2)}) %collective-permute-start.6) | collective-permute-done | bytes 159776 | tf_op jit(solution)/shard_map/ppermute | solution.py:412
  43.5 3.2 %collective-permute-done.7.refs_6_ = bf16[208,384]{1,0:T(8,128)(2,1)S(1)} collective-permute-done((bf16[208,384]{1,0:T(8,128)(2,1)S(1)}, bf16[208,384]{1,0:T(8,128)(2,1)S(1)}, u32[]{:S(2)}, u32[]{:S(2)}) %collective-permute-start.7) | collective-permute-done | bytes 159776 | tf_op jit(solution)/shard_map/ppermute | solution.py:412
  46.8 2.5 %collective-permute-done.8.refs_7_ = bf16[208,384]{1,0:T(8,128)(2,1)S(1)} collective-permute-done((bf16[208,384]{1,0:T(8,128)(2,1)S(1)}, bf16[208,384]{1,0:T(8,128)(2,1)S(1)}, u32[]{:S(2)}, u32[]{:S(2)}) %collective-permute-start.8) | collective-permute-done | bytes 159776 | tf_op jit(solution)/shard_map/ppermute | solution.py:412
  49.3 4.1 %shard_map.148 = bf16[9216,128]{1,0:T(8,128)(2,1)} custom-call(bf16[208,384]{1,0:T(8,128)(2,1)S(1)} %collective-permute-done.1.refs_0_, bf16[208,384]{1,0:T(8,128)(2,1)S(1)} %collective-permute-done.2.refs_1_, bf16[208,384]{1,0:T(8,128)(2,1)S(1)} %collective-permute-done.3.refs_2_, bf16[208,384]{1,0:T(8,128)(2,1)S(1)} %collective-permute-done.4.refs_3_, ...), custom_call_target="tpu_custom_call" | custom-call | flops 5000000000 | bytes 10000000 | tf_op jit(solution)/shard_map/pallas_call | solution.py:331
  53.4 10.5 %all-to-all-start = ((bf16[256,9,4,128]{3,2,1,0:T(4,128)(2,1)}), bf16[256,9,4,128]{3,2,1,0:T(4,128)(2,1)S(1)}, u32[]{:S(2)}, u32[]{:S(2)}) async-start(bf16[256,9,4,128]{3,2,1,0:T(4,128)(2,1)} %bitcast.1), calls=%async_computation | async-start | bytes 4718592 | tf_op jit(solution)/shard_map/all_to_all | solution.py:428
  63.9 0.1 copy.19
  64.1 0.1 maximum_bitcast_fusion.rate_ref
  64.2 0.1 select_maximum_fusion
  64.2 57.4 %all-to-all-done = bf16[256,9,4,128]{3,2,1,0:T(4,128)(2,1)S(1)} async-done(((bf16[256,9,4,128]{3,2,1,0:T(4,128)(2,1)}), bf16[256,9,4,128]{3,2,1,0:T(4,128)(2,1)S(1)}, u32[]{:S(2)}, u32[]{:S(2)}) %all-to-all-start) | async-done | bytes 2359328 | tf_op jit(solution)/shard_map/all_to_all | solution.py:428
  121.6 0.6 copy.18
  122.2 0.4 copy-done
  122.6 0.1 copy-done.1
  122.7 0.1 copy-done.2
  122.9 0.1 copy-done.3
  122.9 9.6 %shard_map.149 = f32[2,6,64,1536]{3,2,1,0:T(8,128)} custom-call(bf16[36,256,128]{2,1,0:T(8,128)(2,1)S(1)} %bitcast.8, f32[6]{0:T(128)S(1)} %multiply_multiply_fusion.wave_ref, bf16[512,256]{1,0:T(8,128)(2,1)S(1)} %copy-done.3, f32[3,256,128]{2,1,0:T(8,128)S(1)} %copy-done.2, f32[3,256,128]{2,1,0:T(8,128)S(1)} %copy-done.1, f32[3,256,128]{2,1,0:T(8,128)S(1)} %copy-done, ...), custom_call_target="tpu_custom_call" | custom-call | tf_op jit(solution)/shard_map/pallas_call | solution.py:455
  (26 shorter events, 0.1 us)
Async XLA Ops:
  0.7 0.8 copy-start.4
  1.5 0.8 copy-start.5
  2.3 0.7 copy-start.6
  5.0 6.9 %collective-permute-start = (bf16[208,384]{1,0:T(8,128)(2,1)S(1)}, bf16[208,384]{1,0:T(8,128)(2,1)S(1)}, u32[]{:S(2)}, u32[]{:S(2)}) collective-permute-start(bf16[208,384]{1,0:T(8,128)(2,1)S(1)} %get-tuple-element.20), channel_id=1, source_target_pairs={{0,8},{8,16},{16,24},{24,32},{32,40},{40,48},{48,56},{56,64},{64,7... | collective-permute-start | bytes 479240 | tf_op jit(solution)/shard_map/ppermute | solution.py:391
  5.1 44.2 %copy-start.7 = (bf16[512,512]{1,0:T(8,128)(2,1)S(1)}, bf16[512,512]{1,0:T(8,128)(2,1)}, u32[]{:S(2)}) copy-start(bf16[512,512]{1,0:T(8,128)(2,1)} %constant.38.clone.refs_8_) | copy-start | bytes 1572868
  5.1 44.2 %copy-start.8 = (f32[3,256,128]{2,1,0:T(8,128)S(1)}, f32[3,256,128]{2,1,0:T(8,128)}, u32[]{:S(2)}) copy-start(f32[3,256,128]{2,1,0:T(8,128)} %constant.41.clone.refs_11_) | copy-start | bytes 1179652
  5.2 44.1 %copy-start.9 = (f32[3,256,128]{2,1,0:T(8,128)S(1)}, f32[3,256,128]{2,1,0:T(8,128)}, u32[]{:S(2)}) copy-start(f32[3,256,128]{2,1,0:T(8,128)} %constant.40.clone.refs_10_) | copy-start | bytes 1179652
  5.2 44.1 %copy-start.10 = (bf16[256,256]{1,0:T(8,128)(2,1)S(1)}, bf16[256,256]{1,0:T(8,128)(2,1)}, u32[]{:S(2)}) copy-start(bf16[256,256]{1,0:T(8,128)(2,1)} %constant.39.clone.refs_9_) | copy-start | bytes 393220
  12.4 15.6 %collective-permute-start.1 = (bf16[208,384]{1,0:T(8,128)(2,1)S(1)}, bf16[208,384]{1,0:T(8,128)(2,1)S(1)}, u32[]{:S(2)}, u32[]{:S(2)}) collective-permute-start(bf16[208,384]{1,0:T(8,128)(2,1)S(1)} %get-tuple-element.21), channel_id=1, source_target_pairs={{0,132},{8,141},{64,196},{72,205},{128,5},{136,12},{192,69},{200,7... | collective-permute-start | bytes 479240 | tf_op jit(solution)/shard_map/ppermute | solution.py:412
  18.2 16.6 %collective-permute-start.2 = (bf16[208,384]{1,0:T(8,128)(2,1)S(1)}, bf16[208,384]{1,0:T(8,128)(2,1)S(1)}, u32[]{:S(2)}, u32[]{:S(2)}) collective-permute-start(bf16[208,384]{1,0:T(8,128)(2,1)S(1)} %get-tuple-element.22), channel_id=1, source_target_pairs={{0,133},{8,140},{64,197},{72,204},{128,4},{136,13},{192,68},{200,7... | collective-permute-start | bytes 479240 | tf_op jit(solution)/shard_map/ppermute | solution.py:412
  20.4 16.0 %collective-permute-start.3 = (bf16[208,384]{1,0:T(8,128)(2,1)S(1)}, bf16[208,384]{1,0:T(8,128)(2,1)S(1)}, u32[]{:S(2)}, u32[]{:S(2)}) collective-permute-start(bf16[208,384]{1,0:T(8,128)(2,1)S(1)} %get-tuple-element.23), channel_id=1, source_target_pairs={{0,130},{8,139},{64,194},{72,203},{128,3},{136,10},{192,67},{200,7... | collective-permute-start | bytes 479240 | tf_op jit(solution)/shard_map/ppermute | solution.py:412
  22.0 17.0 %collective-permute-start.4 = (bf16[208,384]{1,0:T(8,128)(2,1)S(1)}, bf16[208,384]{1,0:T(8,128)(2,1)S(1)}, u32[]{:S(2)}, u32[]{:S(2)}) collective-permute-start(bf16[208,384]{1,0:T(8,128)(2,1)S(1)} %get-tuple-element.24), channel_id=1, source_target_pairs={{0,131},{8,138},{64,195},{72,202},{128,2},{136,11},{192,66},{200,7... | collective-permute-start | bytes 479240 | tf_op jit(solution)/shard_map/ppermute | solution.py:412
  25.0 14.3 %collective-permute-start.5 = (bf16[208,384]{1,0:T(8,128)(2,1)S(1)}, bf16[208,384]{1,0:T(8,128)(2,1)S(1)}, u32[]{:S(2)}, u32[]{:S(2)}) collective-permute-start(bf16[208,384]{1,0:T(8,128)(2,1)S(1)} %get-tuple-element.25), channel_id=1, source_target_pairs={{0,134},{8,143},{64,198},{72,207},{128,7},{136,14},{192,71},{200,7... | collective-permute-start | bytes 479240 | tf_op jit(solution)/shard_map/ppermute | solution.py:412
  28.0 15.6 %collective-permute-start.6 = (bf16[208,384]{1,0:T(8,128)(2,1)S(1)}, bf16[208,384]{1,0:T(8,128)(2,1)S(1)}, u32[]{:S(2)}, u32[]{:S(2)}) collective-permute-start(bf16[208,384]{1,0:T(8,128)(2,1)S(1)} %get-tuple-element.26), channel_id=1, source_target_pairs={{0,135},{8,142},{64,199},{72,206},{128,6},{136,15},{192,70},{200,7... | collective-permute-start | bytes 479240 | tf_op jit(solution)/shard_map/ppermute | solution.py:412
  34.8 12.0 %collective-permute-start.7 = (bf16[208,384]{1,0:T(8,128)(2,1)S(1)}, bf16[208,384]{1,0:T(8,128)(2,1)S(1)}, u32[]{:S(2)}, u32[]{:S(2)}) collective-permute-start(bf16[208,384]{1,0:T(8,128)(2,1)S(1)} %get-tuple-element.27), channel_id=1, source_target_pairs={{0,128},{8,137},{64,192},{72,201},{128,1},{136,8},{192,65},{200,72... | collective-permute-start | bytes 479240 | tf_op jit(solution)/shard_map/ppermute | solution.py:412
  36.4 12.9 %collective-permute-start.8 = (bf16[208,384]{1,0:T(8,128)(2,1)S(1)}, bf16[208,384]{1,0:T(8,128)(2,1)S(1)}, u32[]{:S(2)}, u32[]{:S(2)}) collective-permute-start(bf16[208,384]{1,0:T(8,128)(2,1)S(1)} %get-tuple-element.28), channel_id=1, source_target_pairs={{0,129},{8,136},{64,193},{72,200},{128,0},{136,9},{192,64},{200,73... | collective-permute-start | bytes 479240 | tf_op jit(solution)/shard_map/ppermute | solution.py:412
  53.4 10.5 %copy-start.11 = (f32[64,64]{1,0:T(8,128)S(1)}, f32[64,64]{1,0:T(8,128)}, u32[]{:S(2)}) copy-start(f32[64,64]{1,0:T(8,128)} %param.21) | copy-start | bytes 49156
  53.4 10.7 %copy-start.13 = (f32[64]{0:T(128)S(1)}, f32[64]{0:T(128)}, u32[]{:S(2)}) copy-start(f32[64]{0:T(128)} %param.19) | copy-start | bytes 772
  53.4 10.8 %copy-start.12 = (f32[64,64]{1,0:T(8,128)S(1)}, f32[64,64]{1,0:T(8,128)}, u32[]{:S(2)}) copy-start(f32[64,64]{1,0:T(8,128)} %param.20) | copy-start | bytes 49156
  53.4 68.2 %all-to-all-start = ((bf16[256,9,4,128]{3,2,1,0:T(4,128)(2,1)}), bf16[256,9,4,128]{3,2,1,0:T(4,128)(2,1)S(1)}, u32[]{:S(2)}, u32[]{:S(2)}) async-start(bf16[256,9,4,128]{3,2,1,0:T(4,128)(2,1)} %bitcast.1), calls=%async_computation | async-start | bytes 4718592 | tf_op jit(solution)/shard_map/all_to_all | solution.py:428
  121.6 1.0 copy-start
  121.6 1.1 copy-start.1
  121.6 1.2 copy-start.2
  121.6 1.3 copy-start.3
